TPU v7x, 32 devices: a whole 2x2x4 slice. The times are simulated.
32 devices in a mesh: wide: 4 (over y, x), narrow: 8 (over z, core).
Axes of the slice: x: 2, y: 2, z: 4, core: 2. Of those that a mesh axis runs over, the one named last changes fastest.
Arguments:
- tokens: bfloat16 [16384, 768], P(('wide', 'narrow')), may hold values from -6 to 6
- cotangent: bfloat16 [16384, 768], P(('wide', 'narrow')), may hold values from -6 to 6
- time_emb: bfloat16 [16, 128], replicated, may hold values from -5 to 5
- seq_table: int32 [16], P('wide'), may hold values from 0 to 15, each once
- lengths: int32 [4, 4], P('wide'), may hold values from 1 to 2048, 4096 in all within a row
- positions: int32 [16384], P(('wide', 'narrow')), may hold values from 0 to 8191
- norm1_gain: bfloat16 [768], P('narrow'), may hold values from 0.5 to 1.5
- norm2_gain: bfloat16 [768], P('narrow'), may hold values from 0.5 to 1.5
- ada_weight: bfloat16 [128, 4608], P('narrow'), may hold values from -0.5 to 0.5
- ada_bias: bfloat16 [4608], P('narrow'), may hold values from -3 to 3
- qkv_weight: bfloat16 [768, 2304], P('narrow'), may hold values from -0.21875 to 0.21875
- out_weight: bfloat16 [768, 768], P('narrow'), may hold values from -1.75 to 1.75
- fc1_weight: bfloat16 [768, 3072], P('narrow'), may hold values from -0.21875 to 0.21875
- fc1_bias: bfloat16 [3072], P('narrow'), may hold values from -3 to 3
- fc2_weight: bfloat16 [3072, 768], P('narrow'), may hold values from -0.109375 to 0.109375
- fc2_bias: bfloat16 [768], P('narrow'), may hold values from -5 to 5
Outputs:
- layer_out: bfloat16 [16384, 768], P(('wide', 'narrow'))
- grad_tokens: float32 [16384, 768], P(('wide', 'narrow'))
- grad_time: float32 [16, 128], P('narrow')
- grad_norm1: float32 [768], P('narrow')
- grad_norm2: float32 [768], P('narrow')
- grad_ada_weight: float32 [128, 4608], P('narrow')
- grad_ada_bias: float32 [4608], P('narrow')
- grad_qkv_weight: float32 [768, 2304], P('narrow')
- grad_out_weight: float32 [768, 768], P('narrow')
- grad_fc1_weight: float32 [768, 3072], P('narrow')
- grad_fc1_bias: float32 [3072], P('narrow')
- grad_fc2_weight: float32 [3072, 768], P('narrow')
- grad_fc2_bias: float32 [768], P('narrow')
Inputs may be any that keep to these rules, and one draw needn't show every extreme that they name: `seq_table`: each group's 4 entries name the sequences that fill its slots; every sequence is named once. `lengths`: each row sums to 4096.
All inputs are finite; a program needn't handle non-finite values.
Results may differ from a plain program's by a relative error of at most 0.025.
The roundings to bfloat16 on the way count: a program that leaves them out, or rounds other values in their place, can miss the bound.
Values may be sent and summed in bfloat16 or wider, within the bound.
A program may use at most 192 MiB of HBM per device.

v0:
```python
import functools
import math

import jax
import jax.numpy as jnp
import numpy as np
from jax import lax
from jax.experimental import pallas as pl
from jax.experimental.pallas import tpu as pltpu
from jax.sharding import PartitionSpec as P

HEADS = 12
HEAD_DIM = 64
EPSILON = 1e-05
FAR = -(2.0**100)
F32 = jnp.float32
BF16 = jnp.bfloat16
HIGH = lax.Precision.HIGHEST
VMEM_LIMIT = 56 * 2**20
TILE = 128
QUERY_ROWS = 256
KEY_ROWS = 256
BLOCK = 512


def params(grid_dims=1):
    return pltpu.CompilerParams(
        dimension_semantics=("arbitrary",) * grid_dims, vmem_limit_bytes=VMEM_LIMIT
    )


def dot(left, right, contract=((1,), (0,)), precision=None):
    return lax.dot_general(
        left, right, (contract, ((), ())), preferred_element_type=F32, precision=precision
    )


def thirds(values):
    high = values.astype(BF16)
    rest = values - high.astype(F32)
    middle = rest.astype(BF16)
    low = (rest - middle.astype(F32)).astype(BF16)
    return high, middle, low


def slot_of(rows, info):
    zero = jnp.zeros_like(rows)
    slot = zero
    for which in range(3):
        slot = slot + jnp.where(rows >= info[which], 1, zero)
    return slot


def scalar_slot(row, info):
    slot = jnp.int32(0)
    for which in range(3):
        slot = slot + jnp.where(row >= info[which], 1, 0)
    return slot


def key_range(first, last, info):
    low_slot = scalar_slot(first, info)
    high_slot = scalar_slot(last, info)
    start = jnp.where(
        low_slot == 0, 0, jnp.where(low_slot == 1, info[0], jnp.where(low_slot == 2, info[1], info[2]))
    )
    end = jnp.where(
        high_slot == 0,
        info[0],
        jnp.where(high_slot == 1, info[1], jnp.where(high_slot == 2, info[2], info[3])),
    )
    return start, end


def block_active(block, info, row_count):
    first = info[4]
    start, end = key_range(first, first + row_count - 1, info)
    return jnp.logical_and(block * BLOCK < end, (block + 1) * BLOCK > start)


def slot_picks(row_count, first_row, info):
    rows = first_row + lax.broadcasted_iota(jnp.int32, (row_count, 16), 0)
    lane = lax.broadcasted_iota(jnp.int32, (row_count, 16), 1)
    return jnp.where(
        jnp.logical_and(slot_of(rows, info) == lane % 4, lane < 12), 1.0, 0.0
    ).astype(BF16)


def pick_table(values):
    high, middle, low = thirds(values)
    zero = jnp.zeros_like(high[:4])
    return jnp.concatenate([high[:4], middle[:4], low[:4], zero], axis=0)


def normed(values):
    center = values - jnp.mean(values, axis=1, keepdims=True)
    spread = jnp.mean(center * center, axis=1, keepdims=True)
    inverse = lax.rsqrt(spread + EPSILON)
    return center * inverse, inverse


def rotary_constants():
    half = HEAD_DIM // 2
    inverse = 10000.0 ** (-(np.arange(half, dtype=np.float64) * 2.0) / HEAD_DIM)
    inverse = inverse.astype(np.float32).astype(np.float64)
    tables = []
    for count, step in ((128, 64), (64, 1)):
        angles = (np.arange(count, dtype=np.float64) * step)[:, None] * inverse[None, :]
        full = np.concatenate(
            [np.tile(np.cos(angles), (1, 4)), np.tile(np.sin(angles), (1, 4))], axis=1
        ).astype(np.float32)
        high = full.astype(jnp.bfloat16)
        low = (full - high.astype(np.float32)).astype(jnp.bfloat16)
        tables.append(np.concatenate([high, low], axis=1))
    return tables


def rotary(position_row, coarse_ref, fine_ref):
    count = position_row.shape[1]
    parts = []
    for picks, table in ((position_row // 64, coarse_ref), (position_row % 64, fine_ref)):
        depth = table.shape[0]
        onehot = (lax.broadcasted_iota(jnp.int32, (depth, count), 0) == picks).astype(F32)
        both = dot(onehot.astype(BF16), table[...], ((0,), (0,)))
        parts.append(both[:, :256] + both[:, 256:])
    coarse, fine = parts
    cosine = coarse[:, :128] * fine[:, :128] - coarse[:, 128:] * fine[:, 128:]
    sine = coarse[:, 128:] * fine[:, :128] + coarse[:, :128] * fine[:, 128:]
    lane = lax.broadcasted_iota(jnp.int32, (count, TILE), 1)
    return cosine, jnp.where(lane % 64 < 32, -sine, sine)


def swapped(values):
    lane = lax.broadcasted_iota(jnp.int32, values.shape, 1)
    return jnp.where(
        lane % 64 < 32, pltpu.roll(values, TILE - 32, 1), pltpu.roll(values, 32, 1)
    )


def turn(values, cosine, sine):
    return values * cosine + swapped(values) * sine


def turn_back(values, cosine, sine):
    return values * cosine - swapped(values) * sine


def project_kernel(
    info, x_ref, position_ref, cond_ref, ada_ref, bias_ref, gain_ref, weight_ref, coarse_ref,
    fine_ref, keys_ref, values_ref, first_ref, query_ref, table_ref,
):
    block = pl.program_id(0)
    width = x_ref.shape[1]
    row_count = query_ref.shape[0]

    @pl.when(block == 0)
    def _():
        modulation = dot(cond_ref[...], ada_ref[...]) + bias_ref[...]
        scale = (1.0 + modulation[:, width:]) * gain_ref[...]
        table_ref[:, :width] = pick_table(scale)
        table_ref[:, width:] = pick_table(modulation[:, :width])

    @pl.when(block_active(block, info, row_count))
    def _():
        x = x_ref[...].astype(F32)
        picks = slot_picks(BLOCK, block * BLOCK, info)
        mods = dot(picks, table_ref[...])
        xh, _ = normed(x)
        first = (xh * mods[:, :width] + mods[:, width:]).astype(BF16)
        first_ref[...] = first
        cosine, sine = rotary(position_ref[pl.ds(block, 1), :], coarse_ref, fine_ref)
        keys = dot(first, weight_ref[:, width : 2 * width])
        for tile in range(width // TILE):
            cut = slice(tile * TILE, (tile + 1) * TILE)
            keys_ref[:, cut] = turn(keys[:, cut], cosine, sine).astype(BF16)
        values_ref[...] = dot(first, weight_ref[:, 2 * width :]).astype(BF16)

        @pl.when(block * BLOCK == info[4])
        def _():
            queries = dot(first, weight_ref[:, :width])
            for tile in range(width // TILE):
                cut = slice(tile * TILE, (tile + 1) * TILE)
                turned = turn(queries[:, cut], cosine, sine).astype(BF16)
                query_ref[:, cut] = (turned.astype(F32) * HEAD_DIM**-0.5).astype(BF16)


def project(info, x_all, positions, cond, ada, bias, gain, weight, tables, row_count):
    total, width = x_all.shape
    rows = pl.BlockSpec((BLOCK, width), lambda i, *_: (i, 0))

    def whole(array):
        return pl.BlockSpec(array.shape, lambda i, *_: (0,) * array.ndim)

    shape = jax.ShapeDtypeStruct((total, width), BF16)
    return pl.pallas_call(
        project_kernel,
        grid_spec=pltpu.PrefetchScalarGridSpec(
            num_scalar_prefetch=1,
            grid=(total // BLOCK,),
            in_specs=[
                rows,
                whole(positions),
                whole(cond),
                pl.BlockSpec((ada.shape[0], 2 * width), lambda i, *_: (0, 0)),
                pl.BlockSpec((1, 2 * width), lambda i, *_: (0, 0)),
                whole(gain),
                whole(weight),
                whole(tables[0]),
                whole(tables[1]),
            ],
            out_specs=[
                rows,
                rows,
                rows,
                pl.BlockSpec((row_count, width), lambda i, *_: (0, 0)),
            ],
            scratch_shapes=[pltpu.VMEM((16, 2 * width), BF16)],
        ),
        out_shape=[shape, shape, shape, jax.ShapeDtypeStruct((row_count, width), BF16)],
        compiler_params=params(),
        name="project",
    )(info, x_all, positions, cond, ada, bias, gain, weight, *tables)


def fill_key_features(feature_ref, info):
    total = feature_ref.shape[0]

    @pl.loop(0, total // KEY_ROWS)
    def _(chunk):
        start = pl.multiple_of(chunk * KEY_ROWS, KEY_ROWS)
        rows = start + lax.broadcasted_iota(jnp.int32, (KEY_ROWS, TILE), 0)
        lane = lax.broadcasted_iota(jnp.int32, (KEY_ROWS, TILE), 1)
        slot = slot_of(rows, info)
        masked = jnp.where(slot == lane, 0.0, FAR)
        ones = jnp.where(lane < 8, 1.0, 0.0)
        feature_ref[pl.ds(start, KEY_ROWS), :] = jnp.where(lane < 4, masked, ones).astype(BF16)


def stacked_heads(flipped):
    sub = lax.broadcasted_iota(jnp.int32, flipped.shape, 0)
    zero = jnp.zeros_like(flipped)
    return jnp.concatenate(
        [jnp.where(sub < HEAD_DIM, flipped, zero), jnp.where(sub < HEAD_DIM, zero, flipped)],
        axis=1,
    )


def slot_rows(first, count, info):
    sub = lax.broadcasted_iota(jnp.int32, (TILE, 2 * count), 0)
    lane = lax.broadcasted_iota(jnp.int32, (TILE, 2 * count), 1)
    return jnp.where(slot_of(first + lane % count, info) == sub, 1.0, 0.0), sub


def attend_kernel(info, q_ref, k_ref, v_ref, out_ref, mass_ref, feature_ref, sum_ref):
    @pl.when(pl.program_id(0) == 0)
    def _():
        fill_key_features(feature_ref, info)

    row_count = q_ref.shape[0]
    wide = 2 * QUERY_ROWS
    for part in range(row_count // QUERY_ROWS):
        first = info[4] + part * QUERY_ROWS
        cut = pl.ds(part * QUERY_ROWS, QUERY_ROWS)
        flipped = q_ref[cut, :].astype(F32).T
        onehot, _ = slot_rows(first, QUERY_ROWS, info)
        queries = jnp.concatenate([stacked_heads(flipped), onehot], axis=0).astype(BF16)
        start, end = key_range(first, first + QUERY_ROWS - 1, info)
        sum_ref[...] = jnp.zeros_like(sum_ref)

        def step(chunk, carried):
            most, mass = carried
            rows = pl.ds(pl.multiple_of(chunk * KEY_ROWS, KEY_ROWS), KEY_ROWS)
            keys = jnp.concatenate([k_ref[rows, :], feature_ref[rows, :]], axis=1)
            scores = dot(keys, queries)
            new_most = jnp.maximum(most, jnp.max(scores, axis=0, keepdims=True))
            shrink = jnp.exp(most - new_most)
            weights = jnp.exp(scores - new_most)
            mass = mass * shrink + jnp.sum(weights, axis=0, keepdims=True)
            sum_ref[...] = sum_ref[...] * shrink + dot(
                v_ref[rows, :], weights.astype(BF16), ((0,), (0,))
            )
            return new_most, mass

        most, mass = lax.fori_loop(
            start // KEY_ROWS,
            (end + KEY_ROWS - 1) // KEY_ROWS,
            step,
            (jnp.full((1, wide), FAR * 2, F32), jnp.zeros((1, wide), F32)),
        )
        result = sum_ref[...] / mass
        joined = jnp.concatenate(
            [result[:HEAD_DIM, :QUERY_ROWS], result[HEAD_DIM:, QUERY_ROWS:]], axis=0
        )
        out_ref[cut, :] = joined.T
        mass_ref[0, pl.ds(part, 1), :] = most + jnp.log(mass)


def attend(info, queries, keys, values):
    row_count, width = queries.shape
    total = keys.shape[0]
    pairs = width // TILE
    parts = row_count // QUERY_ROWS
    narrow = pl.BlockSpec((row_count, TILE), lambda i, *_: (0, i))
    tall = pl.BlockSpec((total, TILE), lambda i, *_: (0, i))
    return pl.pallas_call(
        attend_kernel,
        grid_spec=pltpu.PrefetchScalarGridSpec(
            num_scalar_prefetch=1,
            grid=(pairs,),
            in_specs=[narrow, tall, tall],
            out_specs=[
                narrow,
                pl.BlockSpec((1, parts, 2 * QUERY_ROWS), lambda i, *_: (i, 0, 0)),
            ],
            scratch_shapes=[
                pltpu.VMEM((total, TILE), BF16),
                pltpu.VMEM((TILE, 2 * QUERY_ROWS), F32),
            ],
        ),
        out_shape=[
            jax.ShapeDtypeStruct((row_count, width), F32),
            jax.ShapeDtypeStruct((pairs, parts, 2 * QUERY_ROWS), F32),
        ],
        compiler_params=params(),
        name="attend",
    )(info, queries, keys, values)


def attend_back_kernel(
    info, q_ref, k_ref, v_ref, grad_ref, out_ref, mass_ref, dq_ref, dk_ref, dv_ref,
    feature_ref, dk_sum, dv_sum, dq_sum,
):
    @pl.when(pl.program_id(0) == 0)
    def _():
        fill_key_features(feature_ref, info)

    row_count = q_ref.shape[0]
    total = k_ref.shape[0]
    for block in range(total // BLOCK):

        @pl.when(block_active(block, info, row_count))
        def _():
            rows = pl.ds(block * BLOCK, BLOCK)
            dk_sum[rows, :] = jnp.zeros((BLOCK, TILE), F32)
            dv_sum[rows, :] = jnp.zeros((BLOCK, TILE), F32)

    for part in range(row_count // QUERY_ROWS):
        first = info[4] + part * QUERY_ROWS
        cut = pl.ds(part * QUERY_ROWS, QUERY_ROWS)
        q_rows = q_ref[cut, :].astype(F32)
        g_rows = grad_ref[cut, :].astype(F32)
        q_flip = q_rows.T
        g_flip = g_rows.T
        product = g_flip * out_ref[cut, :].T
        delta = jnp.concatenate(
            [
                jnp.sum(product[:HEAD_DIM], axis=0, keepdims=True),
                jnp.sum(product[HEAD_DIM:], axis=0, keepdims=True),
            ],
            axis=1,
        )
        onehot, sub = slot_rows(first, QUERY_ROWS, info)

        def with_parts(base, row):
            for place, piece in enumerate(thirds(-row)):
                base = jnp.where(sub == 4 + place, piece.astype(F32), base)
            return base

        queries = jnp.concatenate(
            [stacked_heads(q_flip), with_parts(onehot, mass_ref[0, pl.ds(part, 1), :])], axis=0
        ).astype(BF16)
        grads = jnp.concatenate(
            [stacked_heads(g_flip), with_parts(jnp.zeros_like(onehot), delta)], axis=0
        ).astype(BF16)
        lane = lax.broadcasted_iota(jnp.int32, (QUERY_ROWS, TILE), 1)

        def stacked(rows):
            zero = jnp.zeros_like(rows)
            return jnp.concatenate(
                [jnp.where(lane < HEAD_DIM, rows, zero), jnp.where(lane < HEAD_DIM, zero, rows)],
                axis=0,
            ).astype(BF16)

        q_stack = stacked(q_rows)
        g_stack = stacked(g_rows)
        start, end = key_range(first, first + QUERY_ROWS - 1, info)
        dq_sum[...] = jnp.zeros_like(dq_sum)

        def step(chunk, carried):
            rows = pl.ds(pl.multiple_of(chunk * KEY_ROWS, KEY_ROWS), KEY_ROWS)
            keys = k_ref[rows, :]
            features = feature_ref[rows, :]
            probs = jnp.exp(dot(jnp.concatenate([keys, features], axis=1), queries))
            change = dot(jnp.concatenate([v_ref[rows, :], features], axis=1), grads)
            grad_scores = (probs * change).astype(BF16)
            dv_sum[rows, :] += dot(probs.astype(BF16), g_stack)
            dk_sum[rows, :] += dot(grad_scores, q_stack)
            dq_sum[...] += dot(keys, grad_scores, ((0,), (0,)))
            return carried

        lax.fori_loop(start // KEY_ROWS, (end + KEY_ROWS - 1) // KEY_ROWS, step, 0)
        result = dq_sum[...]
        joined = jnp.concatenate(
            [result[:HEAD_DIM, :QUERY_ROWS], result[HEAD_DIM:, QUERY_ROWS:]], axis=0
        )
        dq_ref[cut, :] = joined.T * HEAD_DIM**-0.5

    for block in range(total // BLOCK):

        @pl.when(block_active(block, info, row_count))
        def _():
            rows = pl.ds(block * BLOCK, BLOCK)
            dk_ref[rows, :] = dk_sum[rows, :].astype(BF16)
            dv_ref[rows, :] = dv_sum[rows, :].astype(BF16)


def attend_back(info, queries, keys, values, grads, attended, mass):
    row_count, width = queries.shape
    total = keys.shape[0]
    pairs = width // TILE
    parts = row_count // QUERY_ROWS
    narrow = pl.BlockSpec((row_count, TILE), lambda i, *_: (0, i))
    tall = pl.BlockSpec((total, TILE), lambda i, *_: (0, i))
    return pl.pallas_call(
        attend_back_kernel,
        grid_spec=pltpu.PrefetchScalarGridSpec(
            num_scalar_prefetch=1,
            grid=(pairs,),
            in_specs=[
                narrow,
                tall,
                tall,
                narrow,
                narrow,
                pl.BlockSpec((1, parts, 2 * QUERY_ROWS), lambda i, *_: (i, 0, 0)),
            ],
            out_specs=[narrow, tall, tall],
            scratch_shapes=[
                pltpu.VMEM((total, TILE), BF16),
                pltpu.VMEM((total, TILE), F32),
                pltpu.VMEM((total, TILE), F32),
                pltpu.VMEM((TILE, 2 * QUERY_ROWS), F32),
            ],
        ),
        out_shape=[
            jax.ShapeDtypeStruct((row_count, width), F32),
            jax.ShapeDtypeStruct((total, width), BF16),
            jax.ShapeDtypeStruct((total, width), BF16),
        ],
        compiler_params=params(),
        name="attend_back",
    )(info, queries, keys, values, grads, attended, mass)


def slot_sums(first_row, info, values):
    count = values.shape[0]
    rows = first_row + lax.broadcasted_iota(jnp.int32, (8, count), 1)
    which = lax.broadcasted_iota(jnp.int32, (8, count), 0)
    picks = jnp.where(slot_of(rows, info) == which, 1.0, 0.0).astype(BF16)
    high, middle, low = thirds(values)
    return dot(picks, high) + dot(picks, middle) + dot(picks, low)


def mlp_kernel(
    info, x_ref, attended_ref, cot_ref, cond_ref, ada_ref, bias_ref, gain_ref, out_w_ref,
    fc1_ref, fc1_b_ref, fc2_ref, fc2_b_ref,
    layer_ref, g_fc1_ref, g_fc2_ref, g_fc1_b_ref, g_out_ref, g_att_ref, g_mid_ref, small_ref,
    slots_ref,
    mods_ref, second_ref, second_t_ref, grad2_ref, branch_ref, middle_ref, xh_ref, inverse_ref,
    sum2_ref, gsum_ref,
):
    step = pl.program_id(0)
    width = x_ref.shape[1]
    row_count = x_ref.shape[0]
    first_row = info[4]

    def mod(which):
        picks = slot_picks(row_count, first_row, info)
        return dot(picks, mods_ref[:, which * width : (which + 1) * width])

    @pl.when(step == 0)
    def _():
        mods = dot(cond_ref[...], ada_ref[:, 2 * width :]) + bias_ref[:, 2 * width :]
        mods_ref[:, : 4 * width] = pick_table(mods)
        mods_ref[:, 4 * width :] = pick_table(
            (1.0 + mods[:, 2 * width : 3 * width]) * gain_ref[...]
        )
        attended_low = attended_ref[...].astype(BF16)
        branch = dot(attended_low, out_w_ref[...])
        branch_ref[...] = branch
        middle = x_ref[...].astype(F32) + mod(0) * branch
        middle_ref[...] = middle
        xh, inverse = normed(middle)
        xh_ref[...] = xh
        inverse_ref[...] = jnp.broadcast_to(inverse, inverse_ref.shape)
        second = xh * mod(4) + mod(1)
        second_ref[...] = second.astype(BF16)
        second_t_ref[...] = second.T.astype(BF16)
        grad2 = (cot_ref[...].astype(F32) * mod(3)).astype(BF16)
        grad2_ref[...] = grad2
        small_ref[0:1, :] = jnp.sum(grad2.astype(F32), axis=0, keepdims=True)
        sum2_ref[...] = jnp.zeros_like(sum2_ref)
        gsum_ref[...] = jnp.zeros_like(gsum_ref)

    pre = dot(second_ref[...], fc1_ref[...]) + fc1_b_ref[...]
    root = math.sqrt(2.0 / math.pi)
    square = pre * pre
    bend = jnp.tanh(root * pre * (1.0 + 0.044715 * square))
    half = 0.5 * (1.0 + bend)
    act = (pre * half).astype(BF16)
    slope = half + 0.5 * pre * (1.0 - bend * bend) * (root * (1.0 + 0.134145 * square))
    sum2_ref[...] += dot(act, fc2_ref[...])
    grad_act = dot(grad2_ref[...], fc2_ref[...], ((1,), (1,)))
    grad_pre = (grad_act * slope).astype(BF16)
    g_fc1_b_ref[...] = jnp.sum(grad_pre.astype(F32), axis=0, keepdims=True)
    g_fc2_ref[...] = dot(act, grad2_ref[...], ((0,), (0,))).astype(BF16)
    g_fc1_ref[...] = dot(second_t_ref[...], grad_pre).astype(BF16)
    gsum_ref[...] += dot(grad_pre, fc1_ref[...], ((1,), (1,)))

    @pl.when(step == pl.num_programs(0) - 1)
    def _():
        branch2 = sum2_ref[...] + fc2_b_ref[...]
        layer_ref[...] = (middle_ref[...] + mod(3) * branch2).astype(BF16)
        upstream = cot_ref[...].astype(F32)
        slots_ref[:, 3 * width :] = slot_sums(first_row, info, upstream * branch2)
        grad = gsum_ref[...]
        xh = xh_ref[...]
        picks = slot_picks(row_count, first_row, info)
        slots_ref[:, width : 2 * width] = slot_sums(first_row, info, grad)
        moved = grad * xh
        slots_ref[:, 2 * width : 3 * width] = slot_sums(first_row, info, moved * gain_ref[...])
        small_ref[1:2, :] = jnp.sum(moved * (1.0 + mod(2)), axis=0, keepdims=True)
        h = grad * mod(4)
        inverse = inverse_ref[:, 0:1]
        g_mid = upstream + inverse * (
            h - jnp.mean(h, axis=1, keepdims=True) - xh * jnp.mean(h * xh, axis=1, keepdims=True)
        )
        g_mid_ref[...] = g_mid
        slots_ref[:, :width] = slot_sums(first_row, info, g_mid * branch_ref[...])
        g_branch = (g_mid * mod(0)).astype(BF16)
        g_out_ref[...] = dot(attended_ref[...].astype(BF16), g_branch, ((0,), (0,))).astype(BF16)
        g_att_ref[...] = dot(g_branch, out_w_ref[...], ((1,), (1,))).astype(BF16)


def mlp(info, x, attended, cot, cond, ada, bias, gain, out_w, fc1, fc1_b, fc2, fc2_b):
    row_count, width = x.shape
    hidden = fc1.shape[1]
    chunk = 512

    def whole(shape):
        return pl.BlockSpec(shape, lambda i, *_: (0,) * len(shape))

    columns = pl.BlockSpec((width, chunk), lambda i, *_: (0, i))
    lines = pl.BlockSpec((chunk, width), lambda i, *_: (i, 0))
    part = pl.BlockSpec((1, chunk), lambda i, *_: (0, i))
    rows = (row_count, width)
    return pl.pallas_call(
        mlp_kernel,
        grid_spec=pltpu.PrefetchScalarGridSpec(
            num_scalar_prefetch=1,
            grid=(hidden // chunk,),
            in_specs=[
                whole(rows), whole(rows), whole(rows), whole(cond.shape), whole(ada.shape),
                whole(bias.shape), whole(gain.shape), whole(out_w.shape), columns, part, lines,
                whole(fc2_b.shape),
            ],
            out_specs=[
                whole(rows), columns, lines, part, whole(out_w.shape), whole(rows), whole(rows),
                whole((8, width)), whole((8, 4 * width)),
            ],
            scratch_shapes=[
                pltpu.VMEM((16, 5 * width), BF16),
                pltpu.VMEM(rows, BF16),
                pltpu.VMEM((width, row_count), BF16),
                pltpu.VMEM(rows, BF16),
                pltpu.VMEM(rows, F32),
                pltpu.VMEM(rows, F32),
                pltpu.VMEM(rows, F32),
                pltpu.VMEM((row_count, TILE), F32),
                pltpu.VMEM(rows, F32),
                pltpu.VMEM(rows, F32),
            ],
        ),
        out_shape=[
            jax.ShapeDtypeStruct(rows, BF16),
            jax.ShapeDtypeStruct(fc1.shape, BF16),
            jax.ShapeDtypeStruct(fc2.shape, BF16),
            jax.ShapeDtypeStruct((1, hidden), F32),
            jax.ShapeDtypeStruct(out_w.shape, BF16),
            jax.ShapeDtypeStruct(rows, BF16),
            jax.ShapeDtypeStruct(rows, F32),
            jax.ShapeDtypeStruct((8, width), F32),
            jax.ShapeDtypeStruct((8, 4 * width), F32),
        ],
        compiler_params=params(),
        name="mlp",
    )(info, x, attended, cot, cond, ada, bias, gain, out_w, fc1, fc1_b, fc2, fc2_b)


def spread_kernel(
    info, first_ref, dk_ref, dv_ref, dq_ref, weight_ref, position_ref, coarse_ref, fine_ref,
    dx_ref, own_ref, dw_ref, sum_ref,
):
    block = pl.program_id(0)
    row_count, width = dq_ref.shape

    @pl.when(block == 0)
    def _():
        sum_ref[...] = jnp.zeros_like(sum_ref)

    @pl.when(jnp.logical_not(block_active(block, info, row_count)))
    def _():
        dx_ref[...] = jnp.zeros_like(dx_ref)

    @pl.when(block_active(block, info, row_count))
    def _():
        cosine, sine = rotary(position_ref[pl.ds(block, 1), :], coarse_ref, fine_ref)

        def back(ref):
            tiles = []
            for tile in range(width // TILE):
                cut = slice(tile * TILE, (tile + 1) * TILE)
                tiles.append(turn_back(ref[:, cut].astype(F32), cosine, sine).astype(BF16))
            return jnp.concatenate(tiles, axis=1)

        dk = back(dk_ref)
        dv = dv_ref[...]
        first = first_ref[...]
        total = dot(dk, weight_ref[:, width : 2 * width], ((1,), (1,))) + dot(
            dv, weight_ref[:, 2 * width :], ((1,), (1,))
        )
        sum_ref[:, width : 2 * width] += dot(first, dk, ((0,), (0,)))
        sum_ref[:, 2 * width :] += dot(first, dv, ((0,), (0,)))
        dx_ref[...] = total.astype(BF16)

        @pl.when(block * BLOCK == info[4])
        def _():
            dq = back(dq_ref)
            sum_ref[:, :width] += dot(first, dq, ((0,), (0,)))
            own = dot(dq, weight_ref[:, :width], ((1,), (1,)))
            dx_ref[...] = (total + own).astype(BF16)
            own_ref[...] = total + own

    @pl.when(block == pl.num_programs(0) - 1)
    def _():
        dw_ref[...] = sum_ref[...].astype(BF16)


def spread(info, first, dk, dv, dq, weight, positions, tables):
    row_count, width = dq.shape
    total = first.shape[0]
    rows = pl.BlockSpec((BLOCK, width), lambda i, *_: (i, 0))

    def whole(shape):
        return pl.BlockSpec(shape, lambda i, *_: (0,) * len(shape))

    return pl.pallas_call(
        spread_kernel,
        grid_spec=pltpu.PrefetchScalarGridSpec(
            num_scalar_prefetch=1,
            grid=(total // BLOCK,),
            in_specs=[
                rows, rows, rows, whole(dq.shape), whole(weight.shape), whole(positions.shape),
                whole(tables[0].shape), whole(tables[1].shape),
            ],
            out_specs=[rows, whole(dq.shape), whole(weight.shape)],
            scratch_shapes=[pltpu.VMEM(weight.shape, F32)],
        ),
        out_shape=[
            jax.ShapeDtypeStruct((total, width), BF16),
            jax.ShapeDtypeStruct(dq.shape, F32),
            jax.ShapeDtypeStruct(weight.shape, BF16),
        ],
        compiler_params=params(),
        name="spread",
    )(info, first, dk, dv, dq, weight, positions, *tables)


def finish_kernel(
    info, grad_ref, x_ref, g_mid_ref, cond_ref, ada_ref, bias_ref, gain_ref,
    tokens_ref, small_ref, slots_ref,
):
    width = x_ref.shape[1]
    first_row = info[4]
    mods = dot(cond_ref[...], ada_ref[...]) + bias_ref[...]
    scale = 1.0 + mods[:, width:]
    picks = slot_picks(x_ref.shape[0], first_row, info)
    grad = grad_ref[...].astype(F32)
    xh, inverse = normed(x_ref[...].astype(F32))
    slots_ref[:, :width] = slot_sums(first_row, info, grad)
    moved = grad * xh
    slots_ref[:, width:] = slot_sums(first_row, info, moved * gain_ref[...])
    small_ref[0:1, :] = jnp.sum(moved * dot(picks, pick_table(scale)), axis=0, keepdims=True)
    h = grad * dot(picks, pick_table(scale * gain_ref[...]))
    tokens_ref[...] = g_mid_ref[...] + inverse * (
        h - jnp.mean(h, axis=1, keepdims=True) - xh * jnp.mean(h * xh, axis=1, keepdims=True)
    )


def finish(info, grad, x, g_mid, cond, ada, bias, gain):
    row_count, width = x.shape

    def whole(shape):
        return pl.BlockSpec(shape, lambda i, *_: (0,) * len(shape))

    return pl.pallas_call(
        finish_kernel,
        grid_spec=pltpu.PrefetchScalarGridSpec(
            num_scalar_prefetch=1,
            grid=(1,),
            in_specs=[
                whole(grad.shape), whole(x.shape), whole(x.shape), whole(cond.shape),
                whole((ada.shape[0], 2 * width)), whole((1, 2 * width)), whole(gain.shape),
            ],
            out_specs=[whole(x.shape), whole((8, width)), whole((8, 2 * width))],
        ),
        out_shape=[
            jax.ShapeDtypeStruct(x.shape, F32),
            jax.ShapeDtypeStruct((8, width), F32),
            jax.ShapeDtypeStruct((8, 2 * width), F32),
        ],
        compiler_params=params(),
        name="finish",
    )(info, grad, x, g_mid, cond, ada, bias, gain)


def body(
    tokens, cotangent, time_emb, seq_table, lengths, positions, norm1_gain, norm2_gain,
    ada_weight, ada_bias, qkv_weight, out_weight, fc1_weight, fc1_bias, fc2_weight, fc2_bias,
):
    row_count, width = tokens.shape
    me = lax.axis_index("narrow")
    first_row = me * row_count
    slots = lengths.shape[1]
    below = np.tril(np.ones((slots, slots), np.int32))
    seq_ends = jnp.sum(jnp.asarray(below) * lengths[0][None, :], axis=1)
    info = jnp.concatenate(
        [seq_ends, first_row[None], jnp.zeros((3,), jnp.int32)]
    ).astype(jnp.int32)
    onehot_table = (
        seq_table[:, None] == jnp.arange(time_emb.shape[0], dtype=jnp.int32)[None, :]
    ).astype(BF16)
    cond = jnp.dot(onehot_table, time_emb, preferred_element_type=F32).astype(BF16)
    cond8 = jnp.concatenate([cond, jnp.zeros_like(cond)], axis=0)
    tables = tuple(jnp.asarray(t) for t in rotary_constants())

    def gather(shard):
        return lax.all_gather(shard, "narrow", axis=0, tiled=True)

    x_all = gather(tokens)
    position_all = gather(positions.reshape(1, row_count))
    ada = gather(ada_weight)
    qkv_w = gather(qkv_weight)
    out_w = gather(out_weight)
    fc1 = gather(fc1_weight)
    fc2 = gather(fc2_weight)
    vector = gather(jnp.concatenate([norm1_gain, norm2_gain, ada_bias, fc1_bias, fc2_bias])[None])
    cuts = np.cumsum([norm1_gain.size, norm2_gain.size, ada_bias.size, fc1_bias.size])
    gain1, gain2, bias, fc1_b, fc2_b = (
        piece.reshape(1, -1).astype(F32) for piece in jnp.split(vector, cuts, axis=1)
    )

    keys, values, first, queries = project(
        info, x_all, position_all, cond8, ada, bias, gain1, qkv_w, tables, row_count
    )
    attended, mass = attend(info, queries, keys, values)
    layer_out, g_fc1, g_fc2, g_fc1_b, g_out, g_att, g_mid, small2, slots2 = mlp(
        info, tokens, attended, cotangent, cond8, ada, bias, gain2, out_w, fc1, fc1_b, fc2, fc2_b
    )
    dq, dk, dv = attend_back(info, queries, keys, values, g_att, attended, mass)
    dx, own, g_qkv = spread(info, first, dk, dv, dq, qkv_w, position_all, tables)
    grad_first = lax.psum_scatter(dx, "narrow", scatter_dimension=0, tiled=True)
    grad_tokens, small1, slots1 = finish(
        info, grad_first, tokens, g_mid, cond8, ada, bias, gain1
    )
    grad_slot = jnp.concatenate([slots1[:slots], slots2[:slots]], axis=1)
    grad_ada_bias = jnp.sum(grad_slot, axis=0)
    grad_ada = jnp.einsum("sc,se->ce", cond.astype(F32), grad_slot, precision=HIGH)
    grad_cond = jnp.einsum("se,ce->sc", grad_slot, ada.astype(F32), precision=HIGH)
    grad_time = jnp.einsum("sn,sc->nc", onehot_table.astype(F32), grad_cond, precision=HIGH)
    partial = (
        grad_time, small1[0], small2[1], grad_ada, grad_ada_bias, g_qkv, g_out, g_fc1,
        g_fc1_b[0], g_fc2, small2[0],
    )
    shards = tuple(
        lax.psum_scatter(part.astype(BF16), "narrow", scatter_dimension=0, tiled=True)
        for part in partial
    )
    sums = jax.tree.map(lambda part: part.astype(F32), lax.psum(shards, "wide"))
    return (layer_out, grad_tokens) + tuple(sums)


def solution(mesh):
    both = P(("wide", "narrow"), None)
    row = P("narrow")
    table = P("narrow", None)
    return jax.shard_map(
        body,
        mesh=mesh,
        in_specs=(
            both, both, P(), P("wide"), P("wide", None), P(("wide", "narrow")), row, row,
            table, row, table, table, table, row, table, row,
        ),
        out_specs=(both, both, table, row, row, table, row, table, table, table, row, table, row),
        check_vma=False,
    )
```

profile of v0, /device:TPU:0, one launch (start us, length us, event | category | flops | bytes accessed | tf_op | source)
XLA Modules:
  0.0 767.7 jit_solution(17748464766463554313)
XLA Ops:
  11.3 14.4 %all-gather.2 = s32[8,1,512]{2,1,0:T(1,128)S(1)} all-gather(s32[1,1,512]{2,1,0:T(1,128)S(1)} %bitcast.19), channel_id=2, replica_groups=mesh['wide'=4,'narrow'=8] {'narrow'}, dimensions={0}, use_global_device_ids=true | all-gather | bytes 18432 | tf_op jit(solution)/shard_map/all_gather | solution.py:748
  28.8 28.4 %all-reduce.1 = bf16[9984]{0:T(1024)(128)(2,1)S(1)} all-reduce(bf16[9984]{0:T(1024)(128)(2,1)S(1)} %dynamic-update-slice), channel_id=3, replica_groups=mesh['wide'=4,'narrow'=8] {'narrow'}, use_global_device_ids=true, to_apply=%add.1 | all-reduce | flops 9984 | bytes 39936
  61.5 16.7 %all-gather.14.cloned.1.call-done.weight_ref = bf16[768,2304]{1,0:T(8,128)(2,1)} async-done(((bf16[96,2304]{1,0:T(8,128)(2,1)}), bf16[768,2304]{1,0:T(8,128)(2,1)}) %all-gather.14.cloned.1.call-update) | async-done | bytes 3538960 | tf_op jit(solution)/shard_map/all_gather | solution.py:748
  78.2 65.4 %all-gather.10.cloned.1.call-done.x_ref = bf16[4096,768]{1,0:T(8,128)(2,1)} async-done(((bf16[512,768]{1,0:T(8,128)(2,1)}), bf16[4096,768]{1,0:T(8,128)(2,1)}) %all-gather.10.cloned.1.call-update) | async-done | bytes 6291472 | tf_op jit(solution)/shard_map/all_gather | solution.py:748
  143.6 17.3 %project.1 = (bf16[4096,768]{1,0:T(8,128)(2,1)}, bf16[4096,768]{1,0:T(8,128)(2,1)}, bf16[4096,768]{1,0:T(8,128)(2,1)}, bf16[512,768]{1,0:T(8,128)(2,1)}) custom-call(s32[8]{0:T(128)} %pad_add_fusion.info, bf16[4096,768]{1,0:T(8,128)(2,1)} %all-gather.10.cloned.1.call-done.x_ref, s32[8,512]{1,0:T(8,128)} %bitcast.16, bf16[8,128]{1,0:T(8,128)(2,1)} %concatenate.13.cond_ref, ...), custom_call_target="tpu_custom_call" | custom-call | tf_op jit(solution)/shard_map/project/pallas_call | solution.py:195
  160.8 24.3 %attend.1 = (f32[512,768]{1,0:T(8,128)}, f32[6,2,512]{2,1,0:T(2,128)}) custom-call(s32[8]{0:T(128)} %pad_add_fusion.info, bf16[512,768]{1,0:T(8,128)(2,1)} %get-tuple-element.36.q_ref, bf16[4096,768]{1,0:T(8,128)(2,1)} %get-tuple-element.37.k_ref, bf16[4096,768]{1,0:T(8,128)(2,1)} %get-tuple-element.38.v_ref), custom_call_target="tpu_custom_call" | custom-call | tf_op jit(solution)/shard_map/attend/pallas_call | solution.py:305
  185.1 34.3 %all-gather.18.cloned.1.call-done.fc1_ref = bf16[768,3072]{1,0:T(8,128)(2,1)} async-done(((bf16[96,3072]{1,0:T(8,128)(2,1)}), bf16[768,3072]{1,0:T(8,128)(2,1)}) %all-gather.18.cloned.1.call-update) | async-done | bytes 4718608 | tf_op jit(solution)/shard_map/all_gather | solution.py:748
  219.4 52.0 %all-gather.20.cloned.1.call-done.fc2_ref = bf16[3072,768]{1,0:T(8,128)(2,1)} async-done(((bf16[384,768]{1,0:T(8,128)(2,1)}), bf16[3072,768]{1,0:T(8,128)(2,1)}) %all-gather.20.cloned.1.call-update) | async-done | bytes 4718608 | tf_op jit(solution)/shard_map/all_gather | solution.py:748
  271.4 31.3 %mlp.1 = (bf16[512,768]{1,0:T(8,128)(2,1)}, bf16[768,3072]{1,0:T(8,128)(2,1)}, bf16[3072,768]{1,0:T(8,128)(2,1)}, f32[1,3072]{1,0:T(1,128)}, bf16[768,768]{1,0:T...) custom-call(s32[8]{0:T(128)} %pad_add_fusion.info, ...), custom_call_target="tpu_custom_call" | custom-call | tf_op jit(solution)/shard_map/mlp/pallas_call | solution.py:557
  302.7 27.5 %attend_back.1 = (f32[512,768]{1,0:T(8,128)}, bf16[4096,768]{1,0:T(8,128)(2,1)}, bf16[4096,768]{1,0:T(8,128)(2,1)}) custom-call(s32[8]{0:T(128)} %pad_add_fusion.info, bf16[512,768]{1,0:T(8,128)(2,1)} %get-tuple-element.36.q_ref, bf16[4096,768]{1,0:T(8,128)(2,1)} %get-tuple-element.37.k_ref, bf16[4096,768]{1,0:T(8,128)(2,1)} %get-tuple-element.38.v_ref, ...), custom_call_target="tpu_custom_call" | custom-call | tf_op jit(solution)/shard_map/attend_back/pallas_call | solution.py:424
  330.3 22.7 %spread.1 = (bf16[4096,768]{1,0:T(8,128)(2,1)}, f32[512,768]{1,0:T(8,128)}, bf16[768,2304]{1,0:T(8,128)(2,1)}) custom-call(s32[8]{0:T(128)} %pad_add_fusion.info, bf16[4096,768]{1,0:T(8,128)(2,1)} %get-tuple-element.41.first_ref, bf16[4096,768]{1,0:T(8,128)(2,1)} %get-tuple-element.44.dk_ref, bf16[4096,768]{1,0:T(8,128)(2,1)} %get-tuple-element.45.dv_ref, ...), custom_call_target="tpu_custom_call" | custom-call | tf_op jit(solution)/shard_map/spread/pallas_call | solution.py:657
  356.0 104.1 %reduce-scatter.7.cloned.1.call-done.grad_ref = bf16[512,768]{1,0:T(8,128)(2,1)} async-done(((bf16[4096,768]{1,0:T(8,128)(2,1)}), bf16[512,768]{1,0:T(8,128)(2,1)}) %reduce-scatter.7.cloned.1.call-update) | async-done | bytes 786448 | tf_op jit(solution)/shard_map/reduce_scatter | solution.py:772
  460.2 6.0 finish.1
  467.0 2.1 convolution_convert_fusion
  469.2 25.0 %reduce-scatter.13.cloned.1.call-done = bf16[96,768]{1,0:T(8,128)(2,1)} async-done(((bf16[768,768]{1,0:T(8,128)(2,1)}), bf16[96,768]{1,0:T(8,128)(2,1)}) %reduce-scatter.13.cloned.1.call-update) | async-done | bytes 147472 | tf_op jit(solution)/shard_map/reduce_scatter | solution.py:786
  494.2 44.2 %reduce-scatter.11.cloned.1.call-done = bf16[96,2304]{1,0:T(8,128)(2,1)} async-done(((bf16[768,2304]{1,0:T(8,128)(2,1)}), bf16[96,2304]{1,0:T(8,128)(2,1)}) %reduce-scatter.11.cloned.1.call-update) | async-done | bytes 442384 | tf_op jit(solution)/shard_map/reduce_scatter | solution.py:786
  538.5 55.7 %reduce-scatter.15.cloned.1.call-done = bf16[96,3072]{1,0:T(8,128)(2,1)} async-done(((bf16[768,3072]{1,0:T(8,128)(2,1)}), bf16[96,3072]{1,0:T(8,128)(2,1)}) %reduce-scatter.15.cloned.1.call-update) | async-done | bytes 589840 | tf_op jit(solution)/shard_map/reduce_scatter | solution.py:786
  594.2 55.8 %reduce-scatter.17.cloned.1.call-done = bf16[384,768]{1,0:T(8,128)(2,1)} async-done(((bf16[3072,768]{1,0:T(8,128)(2,1)}), bf16[384,768]{1,0:T(8,128)(2,1)}) %reduce-scatter.17.cloned.1.call-update) | async-done | bytes 589840 | tf_op jit(solution)/shard_map/reduce_scatter | solution.py:786
  650.0 33.8 %reduce-scatter.9.cloned.1.call-done = bf16[16,4608]{1,0:T(8,128)(2,1)} async-done(((bf16[128,4608]{1,0:T(8,128)(2,1)}), bf16[16,4608]{1,0:T(8,128)(2,1)}) %reduce-scatter.9.cloned.1.call-update) | async-done | bytes 147472 | tf_op jit(solution)/shard_map/reduce_scatter | solution.py:786
  688.6 26.2 %all-reduce.8 = (bf16[16,128]{1,0:T(8,128)(2,1)S(1)}, bf16[768]{0:T(1024)(128)(2,1)S(1)}, bf16[768]{0:T(1024)(128)(2,1)S(1)}, bf16[4608]{0:T(1024)(128)(2,1)S(1)...) all-reduce(bf16[16,128]{1,0:T(8,128)(2,1)S(1)} %convolution_convert, ...), channel_id=5, replica_groups=mesh['wide'=4,'narrow'=8] {'narrow'}, use_global_device_ids=true, to_apply=%region_2.0.clone | all-reduce | flops 12032 | bytes 48128
  715.2 10.3 %all-reduce.9 = (bf16[2,128]{1,0:T(2,128)(2,1)S(1)}, bf16[96]{0:T(256)(128)(2,1)S(1)}, bf16[96]{0:T(256)(128)(2,1)S(1)}, bf16[576]{0:T(1024)(128)(2,1)S(1)}, bf1...) all-reduce(bf16[2,128]{1,0:T(2,128)(2,1)S(1)} %constant_dynamic-sli, ...), channel_id=1, replica_groups=mesh['wide'=4,'narrow'=8] {'wide'}, use_global_device_ids=true, to_apply=%region_3.0 | all-reduce | flops 1504 | bytes 6016 | tf_op jit(solution)/shard_map/psum | solution.py:789
  728.8 25.7 %all-reduce.13.cloned.1.call-done = (bf16[16,4608]{1,0:T(8,128)(2,1)}, bf16[96,2304]{1,0:T(8,128)(2,1)}, bf16[96,768]{1,0:T(8,128)(2,1)}, bf16[96,3072]{1,0:T(8,128)(2,1)}, bf16[384,768]{1,0:T(8,128)(2,1)}) async-done(((bf16[16,4608]{1,0:T(8,128)(2,1)}, bf16[96,2304]{1,0:T(8,128)(2,1)}, bf16[96,768]{1,0:T(8,128)(2,1)}, bf16[96,3072]{1,0:T(8,128)(2,1)}, bf16[384,768]{1,0:T(8,128)(2,1)}), ...) | async-done | bytes 1916944 | tf_op jit(solution)/shard_map/psum | solution.py:789
  754.5 1.7 convert_element_type.110
  756.2 2.0 convert_element_type.113
  (109 shorter events, 23.2 us)
Async XLA Ops:
  7.2 19.9 %copy-start.11 = (u32[32]{0:T(128)S(1)}, u32[32]{0:T(128)}, u32[]{:S(2)}) copy-start(u32[32]{0:T(128)} %constant.27) | copy-start | bytes 388
  7.2 53.5 %copy-start.12 = (s32[4,4]{1,0:T(4,128)S(1)}, s32[4,4]{1,0:T(4,128)}, u32[]{:S(2)}) copy-start(s32[4,4]{1,0:T(4,128)} %constant.7.clone) | copy-start | bytes 196
  7.2 21.1 %copy-start.14 = (bf16[96]{0:T(256)(128)(2,1)S(1)}, bf16[96]{0:T(256)(128)(2,1)}, u32[]{:S(2)}) copy-start(bf16[96]{0:T(256)(128)(2,1)} %param.25) | copy-start | bytes 580
  7.3 21.1 %copy-start.15 = (bf16[96]{0:T(256)(128)(2,1)S(1)}, bf16[96]{0:T(256)(128)(2,1)}, u32[]{:S(2)}) copy-start(bf16[96]{0:T(256)(128)(2,1)} %param.26) | copy-start | bytes 580
  7.3 21.1 %copy-start.10 = (bf16[576]{0:T(1024)(128)(2,1)S(1)}, bf16[576]{0:T(1024)(128)(2,1)}, u32[]{:S(2)}) copy-start(bf16[576]{0:T(1024)(128)(2,1)} %param.28) | copy-start | bytes 3460
  7.3 21.1 %copy-start.13 = (bf16[384]{0:T(512)(128)(2,1)S(1)}, bf16[384]{0:T(512)(128)(2,1)}, u32[]{:S(2)}) copy-start(bf16[384]{0:T(512)(128)(2,1)} %param.32) | copy-start | bytes 2308
  7.3 21.1 %copy-start.16 = (bf16[96]{0:T(256)(128)(2,1)S(1)}, bf16[96]{0:T(256)(128)(2,1)}, u32[]{:S(2)}) copy-start(bf16[96]{0:T(256)(128)(2,1)} %param.34) | copy-start | bytes 580
  7.3 53.4 %copy-start.17 = (s32[1,4]{1,0:T(1,128)S(1)}, s32[1,4]{1,0:T(1,128)}, u32[]{:S(2)}) copy-start(s32[1,4]{1,0:T(1,128)} %param.23) | copy-start | bytes 52
  7.3 54.1 %all-gather.12.cloned.1.call-start = ((), (), s32[]{:S(2)}) async-start(), calls=%async_computation.7 | async-start | bytes 1327104 | tf_op jit(solution)/shard_map/all_gather | solution.py:748
  8.0 70.2 %all-gather.14.cloned.1.call-start = ((), (), s32[]{:S(2)}) async-start(), calls=%async_computation.8 | async-start | bytes 3981312 | tf_op jit(solution)/shard_map/all_gather | solution.py:748
  8.8 134.8 %all-gather.10.cloned.1.call-start = ((), (), s32[]{:S(2)}) async-start(), calls=%async_computation.6 | async-start | bytes 7077888 | tf_op jit(solution)/shard_map/all_gather | solution.py:748
  9.5 175.6 %all-gather.16.cloned.1.call-start = ((), (), s32[]{:S(2)}) async-start(), calls=%async_computation.9 | async-start | bytes 1327104 | tf_op jit(solution)/shard_map/all_gather | solution.py:748
  10.1 209.3 %all-gather.18.cloned.1.call-start = ((), (), s32[]{:S(2)}) async-start(), calls=%async_computation.10 | async-start | bytes 5308416 | tf_op jit(solution)/shard_map/all_gather | solution.py:748
  10.7 260.8 %all-gather.20.cloned.1.call-start = ((), (), s32[]{:S(2)}) async-start(), calls=%async_computation.11 | async-start | bytes 5308416 | tf_op jit(solution)/shard_map/all_gather | solution.py:748
  11.3 448.9 %reduce-scatter.7.cloned.1.call-start = ((), (), s32[]{:S(2)}) async-start(), calls=%async_computation.12 | async-start | bytes 7077888 | tf_op jit(solution)/shard_map/reduce_scatter | solution.py:772
  353.0 141.2 %reduce-scatter.13.cloned.1.call-start = ((), (), s32[]{:S(2)}) async-start(), calls=%async_computation.15 | async-start | bytes 1327104 | tf_op jit(solution)/shard_map/reduce_scatter | solution.py:786
  353.8 184.7 %reduce-scatter.11.cloned.1.call-start = ((), (), s32[]{:S(2)}) async-start(), calls=%async_computation.14 | async-start | bytes 3981312 | tf_op jit(solution)/shard_map/reduce_scatter | solution.py:786
  354.5 239.7 %reduce-scatter.15.cloned.1.call-start = ((), (), s32[]{:S(2)}) async-start(), calls=%async_computation.16 | async-start | bytes 5308416 | tf_op jit(solution)/shard_map/reduce_scatter | solution.py:786
  355.1 294.9 %reduce-scatter.17.cloned.1.call-start = ((), (), s32[]{:S(2)}) async-start(), calls=%async_computation.17 | async-start | bytes 5308416 | tf_op jit(solution)/shard_map/reduce_scatter | solution.py:786
  355.8 328.0 %reduce-scatter.9.cloned.1.call-start = ((), (), s32[]{:S(2)}) async-start(), calls=%async_computation.13 | async-start | bytes 1327104 | tf_op jit(solution)/shard_map/reduce_scatter | solution.py:786
  469.1 217.3 %copy-start.7 = (f32[8,768]{1,0:T(8,128)S(1)}, f32[8,768]{1,0:T(8,128)}, u32[]{:S(2)}) copy-start(f32[8,768]{1,0:T(8,128)} %get-tuple-element.53) | copy-start | bytes 73732
  469.1 217.4 %copy-start.8 = (f32[1,3072]{1,0:T(1,128)S(1)}, f32[1,3072]{1,0:T(1,128)}, u32[]{:S(2)}) copy-start(f32[1,3072]{1,0:T(1,128)} %get-tuple-element.57) | copy-start | bytes 36868
  469.1 218.2 %copy-start.2 = (bf16[128,4608]{1,0:T(8,128)(2,1)S(1)}, bf16[128,4608]{1,0:T(8,128)(2,1)}, u32[]{:S(2)}) copy-start(bf16[128,4608]{1,0:T(8,128)(2,1)} %all-gather.12.cloned.1.call-done.ada_ref) | copy-start | bytes 3538948
  469.1 285.3 %all-reduce.13.cloned.1.call-start = ((), (), s32[]{:S(2)}) async-start(), calls=%async_computation.18 | async-start | bytes 3833856 | tf_op jit(solution)/shard_map/psum | solution.py:789
  (8 other events, 57.7 us)
Sparse Core Ops, SparseCore 0:
  9.8 25.3 all-gather.11
  36.8 41.3 all-gather.13
  79.8 63.6 all-gather.9
  145.0 21.3 all-gather.15
  167.9 51.4 all-gather.17
  220.9 50.4 all-gather.19
  353.1 107.0 reduce-scatter.6
  463.0 31.1 reduce-scatter.12
  496.6 41.8 reduce-scatter.10
  540.7 53.4 reduce-scatter.14
  596.6 53.3 reduce-scatter.16
  652.8 30.9 reduce-scatter.8
  688.0 66.4 all-reduce.12
where the time goes:
time: 779 us; the launch traced here: 768 us
  waiting for transfers between devices  519 us (67%)
  Pallas kernels  129 us (17%)
  blocking collectives  79.3 us (10%)
  between operations  17.4 us (2%)
  other arithmetic  10.9 us (1%)
    reduce_scatter x5, waiting for transfers between devices, body(): lax.psum_scatter(part.astype(BF16), 'narrow', scatter_dimension=0, tiled=...  215 us
    all_gather x6, waiting for transfers between devices, gather(): return lax.all_gather(shard, 'narrow', axis=0, tiled=True)  168 us
    reduce_scatter x1, waiting for transfers between devices, body(): grad_first = lax.psum_scatter(dx, 'narrow', scatter_dimension=0, tiled=True)  104 us
    unnamed x2, blocking collectives  54.6 us
    pallas_call x1, Pallas kernels, mlp(): pl.pallas_call(mlp_kernel, grid_spec=pltpu.PrefetchScalarGridSpec(num_sca...  31.3 us
    pallas_call x1, Pallas kernels, attend_back(): pl.pallas_call(attend_back_kernel, grid_spec=pltpu.PrefetchScalarGridSpec...  27.5 us
    psum x1, waiting for transfers between devices, body(): sums = jax.tree.map(lambda part: part.astype(F32), lax.psum(shards, 'wide'))  25.7 us
    pallas_call x1, Pallas kernels, attend(): pl.pallas_call(attend_kernel, grid_spec=pltpu.PrefetchScalarGridSpec(num_...  24.3 us
  transfers between devices with their start and end apart: 13, of which 11 were waited for; matrix products, arithmetic and copies ran while one was open for 2% of the time, Pallas kernels for 6%

commit v1 on v0

--- a/solution.py
+++ b/solution.py
@@ -724,6 +724,308 @@
     )(info, grad, x, g_mid, cond, ada, bias, gain)
 
 
+MESH = pl.DeviceIdType.MESH
+
+
+def piece_of(array, which):
+    rows, columns = array
+    if rows >= 192:
+        quarter = rows // 4
+        return which * quarter, quarter, 0, columns
+    if rows % 32 == 0 and (columns // 2) % TILE == 0:
+        return (which % 2) * (rows // 2), rows // 2, (which // 2) * (columns // 2), columns // 2
+    return 0, rows, which * (columns // 4), columns // 4
+
+
+class Place:
+    def __init__(self):
+        self.wide = lax.axis_index("wide")
+        self.narrow = lax.axis_index("narrow")
+        self.z = self.narrow // 2
+        self.core = self.narrow % 2
+        self.quarter = self.wide % 4
+        self.bit1 = 1 + self.core
+        self.bit2 = 2 - self.core
+        self.near = self.z + 1 - 2 * (self.z % 2)
+        low = self.z < 2
+        self.order = (self.near, jnp.where(low, 2, 1), jnp.where(low, 3, 0))
+
+    def flip(self, value, bit):
+        return value + bit * (1 - 2 * ((value // bit) % 2))
+
+    def partner(self, bit):
+        return (self.flip(self.wide, bit), self.narrow)
+
+    def sibling(self):
+        return (self.wide, self.narrow + 1 - 2 * self.core)
+
+    def column(self, narrow):
+        return (self.wide, narrow)
+
+    def up(self):
+        return (self.wide, jnp.minimum(self.narrow + 2, 7))
+
+    def down(self):
+        return (self.wide, jnp.maximum(self.narrow - 2, 0))
+
+
+def greet(place, size):
+    barrier = pltpu.get_barrier_semaphore()
+    for step in range(1, size):
+        pl.semaphore_signal(
+            barrier, inc=1, device_id=place.column((place.narrow + step) % size), device_id_type=MESH
+        )
+    for bit in (1, 2):
+        pl.semaphore_signal(barrier, inc=1, device_id=place.partner(bit), device_id_type=MESH)
+    pl.semaphore_wait(barrier, size + 1)
+
+
+def gather_kernel(shapes, size, *refs):
+    count = len(shapes)
+    shard_refs = refs[:count]
+    x_ref, position_ref, vector_ref = refs[count : count + 3]
+    full_refs = refs[count + 3 : 2 * count + 3]
+    x_all, position_all, vector_all = refs[2 * count + 3 : 2 * count + 6]
+    (
+        own_sems, own_send, own_recv, line_send, line_recv, turn_send, turn_recv, next_send,
+        next_recv, back_send, back_recv, small_send, small_recv,
+    ) = refs[2 * count + 6 :]
+    place = Place()
+    narrow, z, core = place.narrow, place.z, place.core
+    greet(place, size)
+
+    def remote(source, target, send, recv, device):
+        return pltpu.make_async_remote_copy(
+            src_ref=source, dst_ref=target, send_sem=send, recv_sem=recv, device_id=device,
+            device_id_type=MESH,
+        )
+
+    def region(a, owner, which):
+        rows, columns = shapes[a]
+        first_row, row_count, first_column, column_count = piece_of(shapes[a], which)
+        start = pl.multiple_of(owner * rows + first_row, 16)
+        if isinstance(first_column, int):
+            return full_refs[a].at[pl.ds(start, row_count), :]
+        lanes = pl.ds(pl.multiple_of(first_column, TILE), column_count)
+        return full_refs[a].at[pl.ds(start, row_count), lanes]
+
+    def shard(a, owner):
+        rows, _ = shapes[a]
+        return full_refs[a].at[pl.ds(pl.multiple_of(owner * rows, 16), rows), :]
+
+    def own_piece(a):
+        first_row, row_count, first_column, column_count = piece_of(shapes[a], place.quarter)
+        if isinstance(first_row, int) and first_row == 0:
+            rows = slice(None)
+        else:
+            rows = pl.ds(pl.multiple_of(first_row, 16), row_count)
+        if isinstance(first_column, int):
+            return shard_refs[a].at[rows, :]
+        return shard_refs[a].at[rows, pl.ds(pl.multiple_of(first_column, TILE), column_count)]
+
+    block = x_ref.shape[0]
+
+    def tokens_of(owner):
+        return x_all.at[pl.ds(pl.multiple_of(owner * block, 16), block), :]
+
+    owner_of = [zp * 2 + core for zp in place.order]
+    smalls = []
+    for step in range(1, size):
+        device = place.column((narrow + step) % size)
+        smalls.append(
+            remote(vector_ref, vector_all.at[narrow], small_send.at[0, step], small_recv.at[0, step], device)
+        )
+        smalls.append(
+            remote(position_ref, position_all.at[narrow], small_send.at[1, step], small_recv.at[1, step], device)
+        )
+    for copy in smalls:
+        copy.start()
+    local = [
+        pltpu.make_async_copy(vector_ref, vector_all.at[narrow], own_sems.at[count + 1]),
+        pltpu.make_async_copy(position_ref, position_all.at[narrow], own_sems.at[count + 2]),
+        pltpu.make_async_copy(x_ref, tokens_of(narrow), own_sems.at[count]),
+    ]
+    for a in range(count):
+        local.append(pltpu.make_async_copy(shard_refs[a], shard(a, narrow), own_sems.at[a]))
+    for copy in local:
+        copy.start()
+
+    def line_copies(a, owner, source, target):
+        return (
+            remote(source, target, line_send.at[a, owner // 2, 0], line_recv.at[a, owner // 2], place.up()),
+            remote(source, target, line_send.at[a, owner // 2, 1], line_recv.at[a, owner // 2], place.down()),
+        )
+
+    def line_pair(a, owner):
+        if a == count:
+            target = tokens_of(owner)
+            source = target
+        else:
+            target = region(a, owner, place.quarter)
+            source = target
+        return line_copies(a, owner, source, target)
+
+    def own_pair(a):
+        if a == count:
+            return line_copies(a, narrow, x_ref, tokens_of(narrow))
+        return line_copies(a, narrow, own_piece(a), region(a, narrow, place.quarter))
+
+    def own_to_sibling(a):
+        if a == count:
+            return remote(x_ref, tokens_of(narrow), own_send.at[a], own_recv.at[a], place.sibling())
+        return remote(shard_refs[a], shard(a, narrow), own_send.at[a], own_recv.at[a], place.sibling())
+
+    def start_own(a):
+        up, down = own_pair(a)
+        pl.when(z < 3)(up.start)
+        pl.when(z > 0)(down.start)
+        own_to_sibling(a).start()
+
+    def forwards(a, index):
+        zp = place.order[index]
+        if a == count:
+            near = jnp.logical_and(zp - z < 2, z - zp < 2)
+            return (
+                jnp.logical_and(jnp.logical_and(zp < z, z < 3), near),
+                jnp.logical_and(jnp.logical_and(zp > z, z > 0), near),
+            )
+        return jnp.logical_and(zp < z, z < 3), jnp.logical_and(zp > z, z > 0)
+
+    def arrives(index):
+        zp = place.order[index]
+        return jnp.logical_and(zp - z < 3, z - zp < 3)
+
+    def quarters(bit_first):
+        first = place.flip(place.quarter, place.bit1)
+        return first, place.flip(place.quarter, place.bit2), place.flip(first, place.bit2)
+
+    def turn_copy(a, index):
+        target = region(a, owner_of[index], place.quarter)
+        return remote(
+            target, target, turn_send.at[a, index], turn_recv.at[a, index], place.partner(place.bit1)
+        )
+
+    def next_copy(a, index, which):
+        quarter = place.quarter if which == 0 else place.flip(place.quarter, place.bit1)
+        target = region(a, owner_of[index], quarter)
+        return remote(
+            target, target, next_send.at[a, index, which], next_recv.at[a, index, which],
+            place.partner(place.bit2),
+        )
+
+    def back_copy(a, index):
+        if a == count:
+            target = tokens_of(owner_of[index])
+        else:
+            target = shard(a, owner_of[index])
+        return remote(
+            target, target, back_send.at[a, index], back_recv.at[a, index], place.sibling()
+        )
+
+    def on_line(a, index):
+        up, down = line_pair(a, owner_of[index])
+
+        def work():
+            up.wait_recv()
+            goes_up, goes_down = forwards(a, index)
+            pl.when(goes_up)(up.start)
+            pl.when(goes_down)(down.start)
+            if a == count:
+                back_copy(a, index).start()
+            else:
+                turn_copy(a, index).start()
+                next_copy(a, index, 0).start()
+
+        if a == count:
+            pl.when(arrives(index))(work)
+        else:
+            work()
+
+    sequence = [0, 1, count] + list(range(2, count))
+    for a in sequence:
+        start_own(a)
+    for a in sequence:
+        for index in range(3):
+            on_line(a, index)
+        if a != count:
+            for index in range(3):
+                turn_copy(a, index).wait_recv()
+                next_copy(a, index, 1).start()
+    for a in range(count):
+        for index in range(3):
+            next_copy(a, index, 0).wait_recv()
+            next_copy(a, index, 1).wait_recv()
+            back_copy(a, index).start()
+    for a in range(count):
+        for index in range(3):
+            back_copy(a, index).wait_recv()
+    for a in range(count + 1):
+        own_to_sibling(a).wait()
+        up, down = own_pair(a)
+        pl.when(z < 3)(up.wait_send)
+        pl.when(z > 0)(down.wait_send)
+    for index in range(3):
+
+        @pl.when(arrives(index))
+        def _():
+            back_copy(count, index).wait()
+            goes_up, goes_down = forwards(count, index)
+            up, down = line_pair(count, owner_of[index])
+            pl.when(goes_up)(up.wait_send)
+            pl.when(goes_down)(down.wait_send)
+
+        for a in range(count):
+            goes_up, goes_down = forwards(a, index)
+            up, down = line_pair(a, owner_of[index])
+            pl.when(goes_up)(up.wait_send)
+            pl.when(goes_down)(down.wait_send)
+            turn_copy(a, index).wait_send()
+            next_copy(a, index, 0).wait_send()
+            next_copy(a, index, 1).wait_send()
+            back_copy(a, index).wait_send()
+    for copy in local:
+        copy.wait()
+    for copy in smalls:
+        copy.wait()
+
+
+def gather_all(x, positions, vector, shards, size):
+    count = len(shards)
+    shapes = tuple(shard.shape for shard in shards)
+    anywhere = pl.BlockSpec(memory_space=pl.ANY)
+    dma = pltpu.SemaphoreType.DMA
+    out_shape = [
+        jax.ShapeDtypeStruct((size * shard.shape[0], shard.shape[1]), shard.dtype) for shard in shards
+    ] + [
+        jax.ShapeDtypeStruct((size * x.shape[0], x.shape[1]), x.dtype),
+        jax.ShapeDtypeStruct((size, *positions.shape), positions.dtype),
+        jax.ShapeDtypeStruct((size, *vector.shape), vector.dtype),
+    ]
+    return pl.pallas_call(
+        functools.partial(gather_kernel, shapes, size),
+        out_shape=out_shape,
+        in_specs=[anywhere] * (count + 3),
+        out_specs=[anywhere] * (count + 3),
+        scratch_shapes=[
+            dma((count + 3,)),
+            dma((count + 1,)),
+            dma((count + 1,)),
+            dma((count + 1, 4, 2)),
+            dma((count + 1, 4)),
+            dma((count, 3)),
+            dma((count, 3)),
+            dma((count, 3, 2)),
+            dma((count, 3, 2)),
+            dma((count + 1, 3)),
+            dma((count + 1, 3)),
+            dma((2, size)),
+            dma((2, size)),
+        ],
+        compiler_params=pltpu.CompilerParams(collective_id=1, has_side_effects=True),
+        name="gather_all",
+    )(*shards, x, positions, vector)
+
+
 def body(
     tokens, cotangent, time_emb, seq_table, lengths, positions, norm1_gain, norm2_gain,
     ada_weight, ada_bias, qkv_weight, out_weight, fc1_weight, fc1_bias, fc2_weight, fc2_bias,
@@ -744,20 +1046,18 @@
     cond8 = jnp.concatenate([cond, jnp.zeros_like(cond)], axis=0)
     tables = tuple(jnp.asarray(t) for t in rotary_constants())
 
-    def gather(shard):
-        return lax.all_gather(shard, "narrow", axis=0, tiled=True)
-
-    x_all = gather(tokens)
-    position_all = gather(positions.reshape(1, row_count))
-    ada = gather(ada_weight)
-    qkv_w = gather(qkv_weight)
-    out_w = gather(out_weight)
-    fc1 = gather(fc1_weight)
-    fc2 = gather(fc2_weight)
-    vector = gather(jnp.concatenate([norm1_gain, norm2_gain, ada_bias, fc1_bias, fc2_bias])[None])
-    cuts = np.cumsum([norm1_gain.size, norm2_gain.size, ada_bias.size, fc1_bias.size])
+    pieces = (norm1_gain, norm2_gain, ada_bias, fc1_bias, fc2_bias)
+    cuts = np.cumsum([piece.size for piece in pieces])
+    room = -cuts[-1] % (16 * TILE)
+    vector = jnp.concatenate([*pieces, jnp.zeros((room,), BF16)]).reshape(16, TILE)
+    ada, qkv_w, out_w, fc1, fc2, x_all, position_all, vectors = gather_all(
+        tokens, positions.reshape(-1, TILE), vector,
+        (ada_weight, qkv_weight, out_weight, fc1_weight, fc2_weight), lax.axis_size("narrow"),
+    )
+    vectors = vectors.reshape(vectors.shape[0], -1)
+    position_all = position_all.reshape(position_all.shape[0], -1)
     gain1, gain2, bias, fc1_b, fc2_b = (
-        piece.reshape(1, -1).astype(F32) for piece in jnp.split(vector, cuts, axis=1)
+        piece.reshape(1, -1).astype(F32) for piece in jnp.split(vectors[:, : cuts[-1]], cuts[:-1], axis=1)
     )
 
     keys, values, first, queries = project(

time: 779 us -> 730 us (0.937)
  waiting for transfers between devices: 519 us -> 334 us
  Pallas kernels: 129 us -> 307 us
  blocking collectives: 79.3 us -> 36.2 us
    all_gather x6 -> x0, waiting for transfers between devices: 168 us -> none  [gather(): return lax.all_gather(shard, 'narrow', axis=0, tiled=True)]
    pallas_call x0 -> x1, Pallas kernels: none -> 113 us  [gather_all(): pl.pallas_call(functools.partial(gather_kernel, shapes, size), out_shape=...]
    pallas_call x1, Pallas kernels: 24.3 us -> 54.4 us  [attend(): pl.pallas_call(attend_kernel, grid_spec=pltpu.PrefetchScalarGridSpec(num_...]
    pallas_call x1, Pallas kernels: 27.5 us -> 56.5 us  [attend_back(): pl.pallas_call(attend_back_kernel, grid_spec=pltpu.PrefetchScalarGridSpec...]
    unnamed x2 -> x1, blocking collectives: 54.6 us -> 26.1 us
    all_gather x1 -> x0, blocking collectives: 14.4 us -> none  [gather(): return lax.all_gather(shard, 'narrow', axis=0, tiled=True)]
    reduce_scatter x1, waiting for transfers between devices: 104 us -> 91.6 us  [body(): grad_first = lax.psum_scatter(dx, 'narrow', scatter_dimension=0, tiled=True)]
  transfers between devices with their start and end apart: 13 -> 7, of which waited for: 11 -> 7; matrix products, arithmetic and copies ran while one was open for 2% -> 1% of each run, Pallas kernels for 6% -> 1%
where the time goes in v1:
time: 730 us; the launch traced here: 722 us
  waiting for transfers between devices  334 us (46%)
  Pallas kernels  307 us (42%)
  blocking collectives  36.2 us (5%)
  between operations  16.9 us (2%)
  local copies, waits for them, and re-layouts  12.9 us (2%)
  other arithmetic  10.9 us (1%)
    reduce_scatter x5, waiting for transfers between devices, body(): lax.psum_scatter(part.astype(BF16), 'narrow', scatter_dimension=0, tiled=...  215 us
    pallas_call x1, Pallas kernels, gather_all(): pl.pallas_call(functools.partial(gather_kernel, shapes, size), out_shape=...  113 us
    reduce_scatter x1, waiting for transfers between devices, body(): grad_first = lax.psum_scatter(dx, 'narrow', scatter_dimension=0, tiled=True)  91.6 us
    pallas_call x1, Pallas kernels, attend_back(): pl.pallas_call(attend_back_kernel, grid_spec=pltpu.PrefetchScalarGridSpec...  56.5 us
    pallas_call x1, Pallas kernels, attend(): pl.pallas_call(attend_kernel, grid_spec=pltpu.PrefetchScalarGridSpec(num_...  54.4 us
    pallas_call x1, Pallas kernels, mlp(): pl.pallas_call(mlp_kernel, grid_spec=pltpu.PrefetchScalarGridSpec(num_sca...  31.3 us
    pallas_call x1, Pallas kernels, spread(): pl.pallas_call(spread_kernel, grid_spec=pltpu.PrefetchScalarGridSpec(num_...  26.4 us
    unnamed x1, blocking collectives  26.1 us
  transfers between devices with their start and end apart: 7, of which 7 were waited for; matrix products, arithmetic and copies ran while one was open for 1% of the time, Pallas kernels for 1%

profile of v1, /device:TPU:0, one launch (start us, length us, event | category | flops | bytes accessed | tf_op | source)
XLA Modules:
  0.0 721.5 jit_solution(13773554931306668255)
XLA Ops:
  7.3 4.1 concatenate.13
  11.3 112.7 %gather_all.1 = (bf16[128,4608]{1,0:T(8,128)(2,1)}, bf16[768,2304]{1,0:T(8,128)(2,1)}, bf16[768,768]{1,0:T(8,128)(2,1)}, bf16[768,3072]{1,0:T(8,128)(2,1)}, bf16...) custom-call(bf16[16,4608]{1,0:T(8,128)(2,1)} %refs_0_.1, ...), custom_call_target="tpu_custom_call" | custom-call | tf_op jit(solution)/shard_map/gather_all/pallas_call | solution.py:1004
  125.0 1.3 copy.38
  131.0 19.4 %project.1 = (bf16[4096,768]{1,0:T(8,128)(2,1)}, bf16[4096,768]{1,0:T(8,128)(2,1)}, bf16[4096,768]{1,0:T(8,128)(2,1)}, bf16[512,768]{1,0:T(8,128)(2,1)}) custom-call(s32[8]{0:T(128)} %pad_add_fusion.info, bf16[4096,768]{1,0:T(8,128)(2,1)} %get-tuple-element.44.x_ref, s32[8,512]{1,0:T(8,128)} %bitcast.21, bf16[8,128]{1,0:T(8,128)(2,1)} %concatenate.14.cond_ref, ...), custom_call_target="tpu_custom_call" | custom-call | tf_op jit(solution)/shard_map/project/pallas_call | solution.py:195
  150.4 54.4 %attend.1 = (f32[512,768]{1,0:T(8,128)}, f32[6,2,512]{2,1,0:T(2,128)}) custom-call(s32[8]{0:T(128)} %pad_add_fusion.info, bf16[512,768]{1,0:T(8,128)(2,1)} %get-tuple-element.49.q_ref, bf16[4096,768]{1,0:T(8,128)(2,1)} %get-tuple-element.50.k_ref, bf16[4096,768]{1,0:T(8,128)(2,1)} %get-tuple-element.51.v_ref), custom_call_target="tpu_custom_call" | custom-call | tf_op jit(solution)/shard_map/attend/pallas_call | solution.py:305
  204.8 31.3 %mlp.1 = (bf16[512,768]{1,0:T(8,128)(2,1)}, bf16[768,3072]{1,0:T(8,128)(2,1)}, bf16[3072,768]{1,0:T(8,128)(2,1)}, f32[1,3072]{1,0:T(1,128)}, bf16[768,768]{1,0:T...) custom-call(s32[8]{0:T(128)} %pad_add_fusion.info, ...), custom_call_target="tpu_custom_call" | custom-call | tf_op jit(solution)/shard_map/mlp/pallas_call | solution.py:557
  236.1 56.5 %attend_back.1 = (f32[512,768]{1,0:T(8,128)}, bf16[4096,768]{1,0:T(8,128)(2,1)}, bf16[4096,768]{1,0:T(8,128)(2,1)}) custom-call(s32[8]{0:T(128)} %pad_add_fusion.info, bf16[512,768]{1,0:T(8,128)(2,1)} %get-tuple-element.49.q_ref, bf16[4096,768]{1,0:T(8,128)(2,1)} %get-tuple-element.50.k_ref, bf16[4096,768]{1,0:T(8,128)(2,1)} %get-tuple-element.51.v_ref, ...), custom_call_target="tpu_custom_call" | custom-call | tf_op jit(solution)/shard_map/attend_back/pallas_call | solution.py:424
  292.7 26.4 %spread.1 = (bf16[4096,768]{1,0:T(8,128)(2,1)}, f32[512,768]{1,0:T(8,128)}, bf16[768,2304]{1,0:T(8,128)(2,1)}) custom-call(s32[8]{0:T(128)} %pad_add_fusion.info, bf16[4096,768]{1,0:T(8,128)(2,1)} %get-tuple-element.57.first_ref, bf16[4096,768]{1,0:T(8,128)(2,1)} %get-tuple-element.60.dk_ref, bf16[4096,768]{1,0:T(8,128)(2,1)} %get-tuple-element.61.dv_ref, ...), custom_call_target="tpu_custom_call" | custom-call | tf_op jit(solution)/shard_map/spread/pallas_call | solution.py:657
  322.1 91.6 %reduce-scatter.7.cloned.1.call-done.grad_ref = bf16[512,768]{1,0:T(8,128)(2,1)} async-done(((bf16[4096,768]{1,0:T(8,128)(2,1)}), bf16[512,768]{1,0:T(8,128)(2,1)}) %reduce-scatter.7.cloned.1.call-update) | async-done | bytes 786448 | tf_op jit(solution)/shard_map/reduce_scatter | solution.py:1072
  413.7 6.0 finish.1
  420.5 2.1 convolution_convert_fusion
  422.7 25.1 %reduce-scatter.13.cloned.1.call-done = bf16[96,768]{1,0:T(8,128)(2,1)} async-done(((bf16[768,768]{1,0:T(8,128)(2,1)}), bf16[96,768]{1,0:T(8,128)(2,1)}) %reduce-scatter.13.cloned.1.call-update) | async-done | bytes 147472 | tf_op jit(solution)/shard_map/reduce_scatter | solution.py:1086
  447.8 44.3 %reduce-scatter.11.cloned.1.call-done = bf16[96,2304]{1,0:T(8,128)(2,1)} async-done(((bf16[768,2304]{1,0:T(8,128)(2,1)}), bf16[96,2304]{1,0:T(8,128)(2,1)}) %reduce-scatter.11.cloned.1.call-update) | async-done | bytes 442384 | tf_op jit(solution)/shard_map/reduce_scatter | solution.py:1086
  492.1 55.8 %reduce-scatter.15.cloned.1.call-done = bf16[96,3072]{1,0:T(8,128)(2,1)} async-done(((bf16[768,3072]{1,0:T(8,128)(2,1)}), bf16[96,3072]{1,0:T(8,128)(2,1)}) %reduce-scatter.15.cloned.1.call-update) | async-done | bytes 589840 | tf_op jit(solution)/shard_map/reduce_scatter | solution.py:1086
  547.9 55.6 %reduce-scatter.17.cloned.1.call-done = bf16[384,768]{1,0:T(8,128)(2,1)} async-done(((bf16[3072,768]{1,0:T(8,128)(2,1)}), bf16[384,768]{1,0:T(8,128)(2,1)}) %reduce-scatter.17.cloned.1.call-update) | async-done | bytes 589840 | tf_op jit(solution)/shard_map/reduce_scatter | solution.py:1086
  603.5 34.1 %reduce-scatter.9.cloned.1.call-done = bf16[16,4608]{1,0:T(8,128)(2,1)} async-done(((bf16[128,4608]{1,0:T(8,128)(2,1)}), bf16[16,4608]{1,0:T(8,128)(2,1)}) %reduce-scatter.9.cloned.1.call-update) | async-done | bytes 147472 | tf_op jit(solution)/shard_map/reduce_scatter | solution.py:1086
  641.7 1.0 fusion.1
  643.0 26.1 %all-reduce.7 = (bf16[16,128]{1,0:T(8,128)(2,1)S(1)}, bf16[768]{0:T(1024)(128)(2,1)S(1)}, bf16[768]{0:T(1024)(128)(2,1)S(1)}, bf16[4608]{0:T(1024)(128)(2,1)S(1)...) all-reduce(bf16[16,128]{1,0:T(8,128)(2,1)S(1)} %convolution_convert, ...), channel_id=3, replica_groups=mesh['wide'=4,'narrow'=8] {'narrow'}, use_global_device_ids=true, to_apply=%region_2.0.clone | all-reduce | flops 12032 | bytes 48128
  669.5 10.1 %all-reduce.8 = (bf16[2,128]{1,0:T(2,128)(2,1)S(1)}, bf16[96]{0:T(256)(128)(2,1)S(1)}, bf16[96]{0:T(256)(128)(2,1)S(1)}, bf16[576]{0:T(1024)(128)(2,1)S(1)}, bf1...) all-reduce(bf16[2,128]{1,0:T(2,128)(2,1)S(1)} %constant_dynamic-sli, ...), channel_id=1, replica_groups=mesh['wide'=4,'narrow'=8] {'wide'}, use_global_device_ids=true, to_apply=%region_3.0 | all-reduce | flops 1504 | bytes 6016 | tf_op jit(solution)/shard_map/psum | solution.py:1089
  682.9 25.1 %all-reduce.12.cloned.1.call-done = (bf16[16,4608]{1,0:T(8,128)(2,1)}, bf16[96,2304]{1,0:T(8,128)(2,1)}, bf16[96,768]{1,0:T(8,128)(2,1)}, bf16[96,3072]{1,0:T(8,128)(2,1)}, bf16[384,768]{1,0:T(8,128)(2,1)}) async-done(((bf16[16,4608]{1,0:T(8,128)(2,1)}, bf16[96,2304]{1,0:T(8,128)(2,1)}, bf16[96,768]{1,0:T(8,128)(2,1)}, bf16[96,3072]{1,0:T(8,128)(2,1)}, bf16[384,768]{1,0:T(8,128)(2,1)}), ...) | async-done | bytes 1916944 | tf_op jit(solution)/shard_map/psum | solution.py:1089
  708.0 1.7 convert_element_type.110
  709.7 2.0 convert_element_type.113
  712.5 1.1 convert_element_type.115
  713.6 1.1 convert_element_type.119
  (77 shorter events, 15.7 us)
Async XLA Ops:
  7.2 119.1 %copy-start = (bf16[16,128]{1,0:T(8,128)(2,1)S(1)}, bf16[16,128]{1,0:T(8,128)(2,1)}, u32[]{:S(2)}) copy-start(bf16[16,128]{1,0:T(8,128)(2,1)} %param.21) | copy-start | bytes 12292
  7.2 123.1 %copy-start.9 = (s32[4,4]{1,0:T(4,128)S(1)}, s32[4,4]{1,0:T(4,128)}, u32[]{:S(2)}) copy-start(s32[4,4]{1,0:T(4,128)} %constant.6.clone) | copy-start | bytes 196
  7.2 119.1 %copy-start.11 = (s32[4]{0:T(128)S(1)}, s32[4]{0:T(128)}, u32[]{:S(2)}) copy-start(s32[4]{0:T(128)} %param.22) | copy-start | bytes 52
  7.2 123.1 %copy-start.10 = (s32[1,4]{1,0:T(1,128)S(1)}, s32[1,4]{1,0:T(1,128)}, u32[]{:S(2)}) copy-start(s32[1,4]{1,0:T(1,128)} %param.23) | copy-start | bytes 52
  7.2 406.5 %reduce-scatter.7.cloned.1.call-start = ((), (), s32[]{:S(2)}) async-start(), calls=%async_computation.6 | async-start | bytes 7077888 | tf_op jit(solution)/shard_map/reduce_scatter | solution.py:1072
  319.1 128.7 %reduce-scatter.13.cloned.1.call-start = ((), (), s32[]{:S(2)}) async-start(), calls=%async_computation.9 | async-start | bytes 1327104 | tf_op jit(solution)/shard_map/reduce_scatter | solution.py:1086
  319.8 172.3 %reduce-scatter.11.cloned.1.call-start = ((), (), s32[]{:S(2)}) async-start(), calls=%async_computation.8 | async-start | bytes 3981312 | tf_op jit(solution)/shard_map/reduce_scatter | solution.py:1086
  320.5 227.3 %reduce-scatter.15.cloned.1.call-start = ((), (), s32[]{:S(2)}) async-start(), calls=%async_computation.10 | async-start | bytes 5308416 | tf_op jit(solution)/shard_map/reduce_scatter | solution.py:1086
  321.1 282.4 %reduce-scatter.17.cloned.1.call-start = ((), (), s32[]{:S(2)}) async-start(), calls=%async_computation.11 | async-start | bytes 5308416 | tf_op jit(solution)/shard_map/reduce_scatter | solution.py:1086
  321.2 0.9 copy-start.6
  321.7 315.9 %reduce-scatter.9.cloned.1.call-start = ((), (), s32[]{:S(2)}) async-start(), calls=%async_computation.7 | async-start | bytes 1327104 | tf_op jit(solution)/shard_map/reduce_scatter | solution.py:1086
  422.6 215.0 %copy-start.7 = (f32[8,768]{1,0:T(8,128)S(1)}, f32[8,768]{1,0:T(8,128)}, u32[]{:S(2)}) copy-start(f32[8,768]{1,0:T(8,128)} %get-tuple-element.69) | copy-start | bytes 73732
  422.6 215.0 %copy-start.12 = (u32[32]{0:T(128)S(1)}, u32[32]{0:T(128)}, u32[]{:S(2)}) copy-start(u32[32]{0:T(128)} %constant.28) | copy-start | bytes 388
  422.6 218.3 %copy-start.8 = (f32[1,3072]{1,0:T(1,128)S(1)}, f32[1,3072]{1,0:T(1,128)}, u32[]{:S(2)}) copy-start(f32[1,3072]{1,0:T(1,128)} %get-tuple-element.73) | copy-start | bytes 36868
  422.6 219.1 %copy-start.2 = (bf16[128,4608]{1,0:T(8,128)(2,1)S(1)}, bf16[128,4608]{1,0:T(8,128)(2,1)}, u32[]{:S(2)}) copy-start(bf16[128,4608]{1,0:T(8,128)(2,1)} %get-tuple-element.46.ada_ref) | copy-start | bytes 3538948
  422.6 285.3 %all-reduce.12.cloned.1.call-start = ((), (), s32[]{:S(2)}) async-start(), calls=%async_computation.12 | async-start | bytes 3833856 | tf_op jit(solution)/shard_map/psum | solution.py:1089
  708.0 3.8 copy-start.5
  708.0 4.5 copy-start.4
  709.7 3.9 copy-start.3
  712.5 2.2 copy-start.1
Sparse Core Ops, SparseCore 0:
  319.2 94.4 reduce-scatter.6
  416.5 31.2 reduce-scatter.12
  450.1 41.9 reduce-scatter.10
  494.4 53.4 reduce-scatter.14
  550.1 53.3 reduce-scatter.16
  606.3 31.2 reduce-scatter.8
  641.8 66.1 all-reduce.11

commit v2 on v1

--- a/solution.py
+++ b/solution.py
@@ -13,14 +13,18 @@
 HEAD_DIM = 64
 EPSILON = 1e-05
 FAR = -(2.0**100)
+SAFE = 64.0
+LIFT = 20.0
 F32 = jnp.float32
 BF16 = jnp.bfloat16
 HIGH = lax.Precision.HIGHEST
 VMEM_LIMIT = 56 * 2**20
+REDUCE_VMEM = 63 * 2**20
 TILE = 128
 QUERY_ROWS = 256
 KEY_ROWS = 256
 BLOCK = 512
+CHUNK = 768
 
 
 def params(grid_dims=1):
@@ -72,10 +76,19 @@
     return start, end
 
 
-def block_active(block, info, row_count):
-    first = info[4]
-    start, end = key_range(first, first + row_count - 1, info)
-    return jnp.logical_and(block * BLOCK < end, (block + 1) * BLOCK > start)
+def active_range(info):
+    start, end = key_range(info[4], info[4] + BLOCK - 1, info)
+    return start // BLOCK, (end - 1) // BLOCK
+
+
+def block_active(block, info):
+    low, high = active_range(info)
+    return jnp.logical_and(block >= low, block <= high)
+
+
+def active_rows(block, info):
+    low, high = active_range(info)
+    return jnp.clip(block, low, high), 0
 
 
 def slot_picks(row_count, first_row, info):
@@ -115,12 +128,15 @@
     return tables
 
 
-def rotary(position_row, coarse_ref, fine_ref):
-    count = position_row.shape[1]
+def rotary(positions, coarse_ref, fine_ref):
+    count = positions.size
     parts = []
-    for picks, table in ((position_row // 64, coarse_ref), (position_row % 64, fine_ref)):
+    for picks, table in ((positions // 64, coarse_ref), (positions % 64, fine_ref)):
         depth = table.shape[0]
-        onehot = (lax.broadcasted_iota(jnp.int32, (depth, count), 0) == picks).astype(F32)
+        sub = lax.broadcasted_iota(jnp.int32, (depth, TILE), 0)
+        onehot = jnp.concatenate(
+            [(sub == picks[at : at + 1, :]).astype(F32) for at in range(positions.shape[0])], axis=1
+        )
         both = dot(onehot.astype(BF16), table[...], ((0,), (0,)))
         parts.append(both[:, :256] + both[:, 256:])
     coarse, fine = parts
@@ -145,9 +161,34 @@
     return values * cosine - swapped(values) * sine
 
 
+def packed(pieces):
+    starts = np.cumsum([0] + [-(-piece.size // TILE) * TILE for piece in pieces])
+    whole = -(-starts[-1] // (16 * TILE)) * 16 * TILE
+    rows = [
+        jnp.pad(piece, (start, whole - start - piece.size)) for piece, start in zip(pieces, starts)
+    ]
+    return functools.reduce(jnp.add, rows).reshape(-1, TILE)
+
+
+def joined(vector_ref, row, size):
+    devices = vector_ref.shape[0]
+    rows = -(-size // TILE)
+    room = -(-(devices - 1) * size // TILE) + rows
+    total = jnp.zeros((8, room * TILE), F32)
+    for device in range(devices):
+        block = vector_ref[device].astype(F32)
+        lanes = [block[row + at : row + at + 1, :] for at in range(rows)]
+        line = jnp.concatenate(lanes, axis=1)
+        line = jnp.concatenate([line, jnp.zeros((1, (room - rows) * TILE), F32)], axis=1)
+        line = jnp.broadcast_to(line, (8, room * TILE))
+        total = total + (pltpu.roll(line, device * size, 1) if device else line)
+    return total[:1, : devices * size]
+
+
 def project_kernel(
-    info, x_ref, position_ref, cond_ref, ada_ref, bias_ref, gain_ref, weight_ref, coarse_ref,
-    fine_ref, keys_ref, values_ref, first_ref, query_ref, table_ref,
+    sizes, info, x_ref, position_ref, cond_ref, ada_ref, vector_ref, weight_ref, coarse_ref,
+    fine_ref, keys_ref, values_ref, first_ref, query_ref, norm_ref, mods_ref, gain_ref, gain2_ref,
+    bias_ref, fc1_b_ref, fc2_b_ref, table_ref,
 ):
     block = pl.program_id(0)
     width = x_ref.shape[1]
@@ -155,12 +196,28 @@
 
     @pl.when(block == 0)
     def _():
-        modulation = dot(cond_ref[...], ada_ref[...]) + bias_ref[...]
+        row = 0
+        for out_ref, size in zip((gain_ref, gain2_ref, bias_ref, fc1_b_ref, fc2_b_ref), sizes):
+            out_ref[...] = joined(vector_ref, row, size)
+            row += -(-size // TILE)
+        modulation = dot(cond_ref[...], ada_ref[...]) + bias_ref[:, : 2 * width]
+        mods_ref[...] = modulation
         scale = (1.0 + modulation[:, width:]) * gain_ref[...]
         table_ref[:, :width] = pick_table(scale)
         table_ref[:, width:] = pick_table(modulation[:, :width])
-
-    @pl.when(block_active(block, info, row_count))
+        norm_ref[...] = jnp.zeros_like(norm_ref)
+
+    def most_square(values):
+        row = lax.broadcasted_iota(jnp.int32, (width, TILE), 0)
+        lane = lax.broadcasted_iota(jnp.int32, (width, TILE), 1)
+        heads = jnp.where(row // HEAD_DIM == lane, 1.0, 0.0).astype(BF16)
+        return jnp.max(dot((values * values).astype(BF16), heads), axis=0, keepdims=True)
+
+    @pl.when(jnp.logical_not(block_active(block, info)))
+    def _():
+        first_ref[...] = jnp.zeros_like(first_ref)
+
+    @pl.when(block_active(block, info))
     def _():
         x = x_ref[...].astype(F32)
         picks = slot_picks(BLOCK, block * BLOCK, info)
@@ -168,8 +225,9 @@
         xh, _ = normed(x)
         first = (xh * mods[:, :width] + mods[:, width:]).astype(BF16)
         first_ref[...] = first
-        cosine, sine = rotary(position_ref[pl.ds(block, 1), :], coarse_ref, fine_ref)
+        cosine, sine = rotary(position_ref[block], coarse_ref, fine_ref)
         keys = dot(first, weight_ref[:, width : 2 * width])
+        norm_ref[0:1, :] = jnp.maximum(norm_ref[0:1, :], most_square(keys) * 1.02)
         for tile in range(width // TILE):
             cut = slice(tile * TILE, (tile + 1) * TILE)
             keys_ref[:, cut] = turn(keys[:, cut], cosine, sine).astype(BF16)
@@ -184,16 +242,17 @@
                 query_ref[:, cut] = (turned.astype(F32) * HEAD_DIM**-0.5).astype(BF16)
 
 
-def project(info, x_all, positions, cond, ada, bias, gain, weight, tables, row_count):
+def project(info, x_all, positions, cond, ada, vectors, sizes, weight, tables, row_count):
     total, width = x_all.shape
-    rows = pl.BlockSpec((BLOCK, width), lambda i, *_: (i, 0))
+    rows = pl.BlockSpec((BLOCK, width), active_rows)
 
     def whole(array):
         return pl.BlockSpec(array.shape, lambda i, *_: (0,) * array.ndim)
 
     shape = jax.ShapeDtypeStruct((total, width), BF16)
+    lengths = [vectors.shape[0] * size for size in sizes]
     return pl.pallas_call(
-        project_kernel,
+        functools.partial(project_kernel, sizes),
         grid_spec=pltpu.PrefetchScalarGridSpec(
             num_scalar_prefetch=1,
             grid=(total // BLOCK,),
@@ -202,8 +261,7 @@
                 whole(positions),
                 whole(cond),
                 pl.BlockSpec((ada.shape[0], 2 * width), lambda i, *_: (0, 0)),
-                pl.BlockSpec((1, 2 * width), lambda i, *_: (0, 0)),
-                whole(gain),
+                whole(vectors),
                 whole(weight),
                 whole(tables[0]),
                 whole(tables[1]),
@@ -211,15 +269,23 @@
             out_specs=[
                 rows,
                 rows,
-                rows,
+                pl.BlockSpec((BLOCK, width), lambda i, *_: (i, 0)),
                 pl.BlockSpec((row_count, width), lambda i, *_: (0, 0)),
-            ],
+                pl.BlockSpec((8, TILE), lambda i, *_: (0, 0)),
+                pl.BlockSpec((8, 2 * width), lambda i, *_: (0, 0)),
+            ]
+            + [pl.BlockSpec((1, count), lambda i, *_: (0, 0)) for count in lengths],
             scratch_shapes=[pltpu.VMEM((16, 2 * width), BF16)],
         ),
-        out_shape=[shape, shape, shape, jax.ShapeDtypeStruct((row_count, width), BF16)],
+        out_shape=[
+            shape, shape, shape, jax.ShapeDtypeStruct((row_count, width), BF16),
+            jax.ShapeDtypeStruct((8, TILE), F32),
+            jax.ShapeDtypeStruct((8, 2 * width), F32),
+        ]
+        + [jax.ShapeDtypeStruct((1, count), F32) for count in lengths],
         compiler_params=params(),
         name="project",
-    )(info, x_all, positions, cond, ada, bias, gain, weight, *tables)
+    )(info, x_all, positions, cond, ada, vectors, weight, *tables)
 
 
 def fill_key_features(feature_ref, info):
@@ -251,51 +317,132 @@
     return jnp.where(slot_of(first + lane % count, info) == sub, 1.0, 0.0), sub
 
 
-def attend_kernel(info, q_ref, k_ref, v_ref, out_ref, mass_ref, feature_ref, sum_ref):
-    @pl.when(pl.program_id(0) == 0)
+def spans(low, count, step, carried, most):
+    span = most
+    while span:
+        times = count // span
+        carried = lax.fori_loop(0, times, functools.partial(step, span, low), carried)
+        low = low + times * span
+        count = count - times * span
+        span //= 2
+    return carried
+
+
+def chunk_rows(chunk):
+    return pl.ds(pl.multiple_of(chunk * KEY_ROWS, KEY_ROWS), KEY_ROWS)
+
+
+def with_parts(base, sub, row):
+    for place, piece in enumerate(thirds(row)):
+        base = jnp.where(sub == 4 + place, piece.astype(F32), base)
+    return base
+
+
+def attend_kernel(
+    info, q_ref, k_ref, v_ref, norm_ref, out_ref, mass_ref, feature_ref, sum_ref, row_ref
+):
+    pair = pl.program_id(0)
+
+    @pl.when(pair == 0)
     def _():
         fill_key_features(feature_ref, info)
 
     row_count = q_ref.shape[0]
     wide = 2 * QUERY_ROWS
+    head = lax.broadcasted_iota(jnp.int32, (1, TILE), 1)
+    longest = [
+        jnp.sqrt(jnp.max(jnp.where(head == 2 * pair + which, norm_ref[0:1, :], 0.0), axis=1, keepdims=True))
+        for which in range(2)
+    ]
     for part in range(row_count // QUERY_ROWS):
         first = info[4] + part * QUERY_ROWS
         cut = pl.ds(part * QUERY_ROWS, QUERY_ROWS)
         flipped = q_ref[cut, :].astype(F32).T
-        onehot, _ = slot_rows(first, QUERY_ROWS, info)
-        queries = jnp.concatenate([stacked_heads(flipped), onehot], axis=0).astype(BF16)
+        onehot, sub = slot_rows(first, QUERY_ROWS, info)
+        stack = stacked_heads(flipped)
         start, end = key_range(first, first + QUERY_ROWS - 1, info)
+        low = start // KEY_ROWS
+        count = (end + KEY_ROWS - 1) // KEY_ROWS - low
         sum_ref[...] = jnp.zeros_like(sum_ref)
 
-        def step(chunk, carried):
-            most, mass = carried
-            rows = pl.ds(pl.multiple_of(chunk * KEY_ROWS, KEY_ROWS), KEY_ROWS)
-            keys = jnp.concatenate([k_ref[rows, :], feature_ref[rows, :]], axis=1)
-            scores = dot(keys, queries)
-            new_most = jnp.maximum(most, jnp.max(scores, axis=0, keepdims=True))
-            shrink = jnp.exp(most - new_most)
-            weights = jnp.exp(scores - new_most)
-            mass = mass * shrink + jnp.sum(weights, axis=0, keepdims=True)
-            sum_ref[...] = sum_ref[...] * shrink + dot(
-                v_ref[rows, :], weights.astype(BF16), ((0,), (0,))
+        def scores_of(rows, queries):
+            return dot(jnp.concatenate([k_ref[rows, :], feature_ref[rows, :]], axis=1), queries)
+
+        own_rows = chunk_rows(first // KEY_ROWS)
+        near = jnp.max(
+            scores_of(own_rows, jnp.concatenate([stack, onehot], axis=0).astype(BF16)),
+            axis=0, keepdims=True,
+        )
+        square = flipped * flipped
+        bound = jnp.concatenate(
+            [
+                jnp.sqrt(jnp.sum(square[:HEAD_DIM], axis=0, keepdims=True)) * longest[0],
+                jnp.sqrt(jnp.sum(square[HEAD_DIM:], axis=0, keepdims=True)) * longest[1],
+            ],
+            axis=1,
+        )
+        shift = near + LIFT
+        narrow_range = jnp.max(bound - shift) < SAFE
+        queries = jnp.concatenate([stack, with_parts(onehot, sub, -shift)], axis=0).astype(BF16)
+
+        @pl.when(narrow_range)
+        def _():
+            def step(span, base, index, mass):
+                weights, values = [], []
+                for inner in range(span):
+                    rows = chunk_rows(base + index * span + inner)
+                    part_weights = jnp.exp(scores_of(rows, queries))
+                    mass = mass + jnp.sum(part_weights, axis=0, keepdims=True)
+                    weights.append(part_weights.astype(BF16))
+                    values.append(v_ref[rows, :])
+                sum_ref[...] += dot(
+                    jnp.concatenate(values, axis=0), jnp.concatenate(weights, axis=0), ((0,), (0,))
+                )
+                return mass
+
+            row_ref[0:1, :] = shift
+            row_ref[1:2, :] = spans(low, count, step, jnp.zeros((1, wide), F32), 8)
+
+        @pl.when(jnp.logical_not(narrow_range))
+        def _():
+            def step(span, base, index, carried):
+                most, mass = carried
+                scores, values = [], []
+                new_most = most
+                for inner in range(span):
+                    rows = chunk_rows(base + index * span + inner)
+                    some = scores_of(rows, queries)
+                    new_most = jnp.maximum(new_most, jnp.max(some, axis=0, keepdims=True))
+                    scores.append(some)
+                    values.append(v_ref[rows, :])
+                shrink = jnp.exp(most - new_most)
+                mass = mass * shrink
+                weights = []
+                for some in scores:
+                    part_weights = jnp.exp(some - new_most)
+                    mass = mass + jnp.sum(part_weights, axis=0, keepdims=True)
+                    weights.append(part_weights.astype(BF16))
+                sum_ref[...] = sum_ref[...] * shrink + dot(
+                    jnp.concatenate(values, axis=0), jnp.concatenate(weights, axis=0), ((0,), (0,))
+                )
+                return new_most, mass
+
+            most, mass = spans(
+                low, count, step, (jnp.full((1, wide), FAR * 2, F32), jnp.zeros((1, wide), F32)), 4
             )
-            return new_most, mass
-
-        most, mass = lax.fori_loop(
-            start // KEY_ROWS,
-            (end + KEY_ROWS - 1) // KEY_ROWS,
-            step,
-            (jnp.full((1, wide), FAR * 2, F32), jnp.zeros((1, wide), F32)),
-        )
+            row_ref[0:1, :] = most + shift
+            row_ref[1:2, :] = mass
+
+        mass = row_ref[1:2, :]
         result = sum_ref[...] / mass
         joined = jnp.concatenate(
             [result[:HEAD_DIM, :QUERY_ROWS], result[HEAD_DIM:, QUERY_ROWS:]], axis=0
         )
         out_ref[cut, :] = joined.T
-        mass_ref[0, pl.ds(part, 1), :] = most + jnp.log(mass)
-
-
-def attend(info, queries, keys, values):
+        mass_ref[0, pl.ds(part, 1), :] = row_ref[0:1, :] + jnp.log(mass)
+
+
+def attend(info, queries, keys, values, norms):
     row_count, width = queries.shape
     total = keys.shape[0]
     pairs = width // TILE
@@ -307,7 +454,7 @@
         grid_spec=pltpu.PrefetchScalarGridSpec(
             num_scalar_prefetch=1,
             grid=(pairs,),
-            in_specs=[narrow, tall, tall],
+            in_specs=[narrow, tall, tall, pl.BlockSpec(norms.shape, lambda i, *_: (0, 0))],
             out_specs=[
                 narrow,
                 pl.BlockSpec((1, parts, 2 * QUERY_ROWS), lambda i, *_: (i, 0, 0)),
@@ -315,6 +462,7 @@
             scratch_shapes=[
                 pltpu.VMEM((total, TILE), BF16),
                 pltpu.VMEM((TILE, 2 * QUERY_ROWS), F32),
+                pltpu.VMEM((8, 2 * QUERY_ROWS), F32),
             ],
         ),
         out_shape=[
@@ -323,7 +471,7 @@
         ],
         compiler_params=params(),
         name="attend",
-    )(info, queries, keys, values)
+    )(info, queries, keys, values, norms)
 
 
 def attend_back_kernel(
@@ -336,9 +484,10 @@
 
     row_count = q_ref.shape[0]
     total = k_ref.shape[0]
+    low_block, high_block = active_range(info)
     for block in range(total // BLOCK):
 
-        @pl.when(block_active(block, info, row_count))
+        @pl.when(jnp.logical_and(block >= low_block, block <= high_block))
         def _():
             rows = pl.ds(block * BLOCK, BLOCK)
             dk_sum[rows, :] = jnp.zeros((BLOCK, TILE), F32)
@@ -361,16 +510,11 @@
         )
         onehot, sub = slot_rows(first, QUERY_ROWS, info)
 
-        def with_parts(base, row):
-            for place, piece in enumerate(thirds(-row)):
-                base = jnp.where(sub == 4 + place, piece.astype(F32), base)
-            return base
-
         queries = jnp.concatenate(
-            [stacked_heads(q_flip), with_parts(onehot, mass_ref[0, pl.ds(part, 1), :])], axis=0
+            [stacked_heads(q_flip), with_parts(onehot, sub, -mass_ref[0, pl.ds(part, 1), :])], axis=0
         ).astype(BF16)
         grads = jnp.concatenate(
-            [stacked_heads(g_flip), with_parts(jnp.zeros_like(onehot), delta)], axis=0
+            [stacked_heads(g_flip), with_parts(jnp.zeros_like(onehot), sub, -delta)], axis=0
         ).astype(BF16)
         lane = lax.broadcasted_iota(jnp.int32, (QUERY_ROWS, TILE), 1)
 
@@ -386,19 +530,26 @@
         start, end = key_range(first, first + QUERY_ROWS - 1, info)
         dq_sum[...] = jnp.zeros_like(dq_sum)
 
-        def step(chunk, carried):
-            rows = pl.ds(pl.multiple_of(chunk * KEY_ROWS, KEY_ROWS), KEY_ROWS)
-            keys = k_ref[rows, :]
-            features = feature_ref[rows, :]
-            probs = jnp.exp(dot(jnp.concatenate([keys, features], axis=1), queries))
-            change = dot(jnp.concatenate([v_ref[rows, :], features], axis=1), grads)
-            grad_scores = (probs * change).astype(BF16)
-            dv_sum[rows, :] += dot(probs.astype(BF16), g_stack)
-            dk_sum[rows, :] += dot(grad_scores, q_stack)
-            dq_sum[...] += dot(keys, grad_scores, ((0,), (0,)))
+        def step(span, base, index, carried):
+            all_keys, all_grads = [], []
+            for inner in range(span):
+                rows = chunk_rows(base + index * span + inner)
+                keys = k_ref[rows, :]
+                features = feature_ref[rows, :]
+                probs = jnp.exp(dot(jnp.concatenate([keys, features], axis=1), queries))
+                change = dot(jnp.concatenate([v_ref[rows, :], features], axis=1), grads)
+                grad_scores = (probs * change).astype(BF16)
+                dv_sum[rows, :] += dot(probs.astype(BF16), g_stack)
+                dk_sum[rows, :] += dot(grad_scores, q_stack)
+                all_keys.append(keys)
+                all_grads.append(grad_scores)
+            dq_sum[...] += dot(
+                jnp.concatenate(all_keys, axis=0), jnp.concatenate(all_grads, axis=0), ((0,), (0,))
+            )
             return carried
 
-        lax.fori_loop(start // KEY_ROWS, (end + KEY_ROWS - 1) // KEY_ROWS, step, 0)
+        low = start // KEY_ROWS
+        spans(low, (end + KEY_ROWS - 1) // KEY_ROWS - low, step, 0, 8)
         result = dq_sum[...]
         joined = jnp.concatenate(
             [result[:HEAD_DIM, :QUERY_ROWS], result[HEAD_DIM:, QUERY_ROWS:]], axis=0
@@ -407,11 +558,17 @@
 
     for block in range(total // BLOCK):
 
-        @pl.when(block_active(block, info, row_count))
+        @pl.when(jnp.logical_and(block >= low_block, block <= high_block))
         def _():
             rows = pl.ds(block * BLOCK, BLOCK)
             dk_ref[rows, :] = dk_sum[rows, :].astype(BF16)
             dv_ref[rows, :] = dv_sum[rows, :].astype(BF16)
+
+        @pl.when(jnp.logical_or(block < low_block, block > high_block))
+        def _():
+            rows = pl.ds(block * BLOCK, BLOCK)
+            dk_ref[rows, :] = jnp.zeros((BLOCK, TILE), BF16)
+            dv_ref[rows, :] = jnp.zeros((BLOCK, TILE), BF16)
 
 
 def attend_back(info, queries, keys, values, grads, attended, mass):
@@ -464,9 +621,8 @@
 def mlp_kernel(
     info, x_ref, attended_ref, cot_ref, cond_ref, ada_ref, bias_ref, gain_ref, out_w_ref,
     fc1_ref, fc1_b_ref, fc2_ref, fc2_b_ref,
-    layer_ref, g_fc1_ref, g_fc2_ref, g_fc1_b_ref, g_out_ref, g_att_ref, g_mid_ref, small_ref,
-    slots_ref,
-    mods_ref, second_ref, second_t_ref, grad2_ref, branch_ref, middle_ref, xh_ref, inverse_ref,
+    layer_ref, g_fc1_ref, g_fc2_ref, g_out_ref, g_att_ref, g_mid_ref, early_ref,
+    pack_ref, mods_ref, second_ref, second_t_ref, grad2_ref, branch_ref, middle_ref, xh_ref, inverse_ref,
     sum2_ref, gsum_ref,
 ):
     step = pl.program_id(0)
@@ -498,7 +654,13 @@
         second_t_ref[...] = second.T.astype(BF16)
         grad2 = (cot_ref[...].astype(F32) * mod(3)).astype(BF16)
         grad2_ref[...] = grad2
-        small_ref[0:1, :] = jnp.sum(grad2.astype(F32), axis=0, keepdims=True)
+        pack_ref[...] = jnp.zeros_like(pack_ref)
+        pack_ref[17:18, :] = jnp.sum(grad2.astype(F32), axis=0, keepdims=True)
+        lane = lax.broadcasted_iota(jnp.int32, (1, width), 1)
+        table = jnp.zeros((1, width), F32)
+        for slot in range(4):
+            table = jnp.where(lane == slot, info[8 + slot].astype(F32), table)
+        pack_ref[22:23, :] = table
         sum2_ref[...] = jnp.zeros_like(sum2_ref)
         gsum_ref[...] = jnp.zeros_like(gsum_ref)
 
@@ -512,7 +674,7 @@
     sum2_ref[...] += dot(act, fc2_ref[...])
     grad_act = dot(grad2_ref[...], fc2_ref[...], ((1,), (1,)))
     grad_pre = (grad_act * slope).astype(BF16)
-    g_fc1_b_ref[...] = jnp.sum(grad_pre.astype(F32), axis=0, keepdims=True)
+    pack_ref[pl.ds(18 + step, 1), :] = jnp.sum(grad_pre.astype(F32), axis=0, keepdims=True)
     g_fc2_ref[...] = dot(act, grad2_ref[...], ((0,), (0,))).astype(BF16)
     g_fc1_ref[...] = dot(second_t_ref[...], grad_pre).astype(BF16)
     gsum_ref[...] += dot(grad_pre, fc1_ref[...], ((1,), (1,)))
@@ -522,21 +684,22 @@
         branch2 = sum2_ref[...] + fc2_b_ref[...]
         layer_ref[...] = (middle_ref[...] + mod(3) * branch2).astype(BF16)
         upstream = cot_ref[...].astype(F32)
-        slots_ref[:, 3 * width :] = slot_sums(first_row, info, upstream * branch2)
+        pack_ref[12:16, :] = slot_sums(first_row, info, upstream * branch2)[:4]
         grad = gsum_ref[...]
         xh = xh_ref[...]
         picks = slot_picks(row_count, first_row, info)
-        slots_ref[:, width : 2 * width] = slot_sums(first_row, info, grad)
+        pack_ref[4:8, :] = slot_sums(first_row, info, grad)[:4]
         moved = grad * xh
-        slots_ref[:, 2 * width : 3 * width] = slot_sums(first_row, info, moved * gain_ref[...])
-        small_ref[1:2, :] = jnp.sum(moved * (1.0 + mod(2)), axis=0, keepdims=True)
+        pack_ref[8:12, :] = slot_sums(first_row, info, moved * gain_ref[...])[:4]
+        pack_ref[16:17, :] = jnp.sum(moved * (1.0 + mod(2)), axis=0, keepdims=True)
         h = grad * mod(4)
         inverse = inverse_ref[:, 0:1]
         g_mid = upstream + inverse * (
             h - jnp.mean(h, axis=1, keepdims=True) - xh * jnp.mean(h * xh, axis=1, keepdims=True)
         )
         g_mid_ref[...] = g_mid
-        slots_ref[:, :width] = slot_sums(first_row, info, g_mid * branch_ref[...])
+        pack_ref[0:4, :] = slot_sums(first_row, info, g_mid * branch_ref[...])[:4]
+        early_ref[...] = pack_ref[...].astype(BF16)
         g_branch = (g_mid * mod(0)).astype(BF16)
         g_out_ref[...] = dot(attended_ref[...].astype(BF16), g_branch, ((0,), (0,))).astype(BF16)
         g_att_ref[...] = dot(g_branch, out_w_ref[...], ((1,), (1,))).astype(BF16)
@@ -545,7 +708,7 @@
 def mlp(info, x, attended, cot, cond, ada, bias, gain, out_w, fc1, fc1_b, fc2, fc2_b):
     row_count, width = x.shape
     hidden = fc1.shape[1]
-    chunk = 512
+    chunk = CHUNK
 
     def whole(shape):
         return pl.BlockSpec(shape, lambda i, *_: (0,) * len(shape))
@@ -565,10 +728,11 @@
                 whole(fc2_b.shape),
             ],
             out_specs=[
-                whole(rows), columns, lines, part, whole(out_w.shape), whole(rows), whole(rows),
-                whole((8, width)), whole((8, 4 * width)),
+                whole(rows), columns, lines, whole(out_w.shape), whole(rows), whole(rows),
+                whole((32, width)),
             ],
             scratch_shapes=[
+                pltpu.VMEM((32, width), F32),
                 pltpu.VMEM((16, 5 * width), BF16),
                 pltpu.VMEM(rows, BF16),
                 pltpu.VMEM((width, row_count), BF16),
@@ -585,156 +749,30 @@
             jax.ShapeDtypeStruct(rows, BF16),
             jax.ShapeDtypeStruct(fc1.shape, BF16),
             jax.ShapeDtypeStruct(fc2.shape, BF16),
-            jax.ShapeDtypeStruct((1, hidden), F32),
             jax.ShapeDtypeStruct(out_w.shape, BF16),
             jax.ShapeDtypeStruct(rows, BF16),
             jax.ShapeDtypeStruct(rows, F32),
-            jax.ShapeDtypeStruct((8, width), F32),
-            jax.ShapeDtypeStruct((8, 4 * width), F32),
+            jax.ShapeDtypeStruct((32, width), BF16),
         ],
         compiler_params=params(),
         name="mlp",
     )(info, x, attended, cot, cond, ada, bias, gain, out_w, fc1, fc1_b, fc2, fc2_b)
 
 
-def spread_kernel(
-    info, first_ref, dk_ref, dv_ref, dq_ref, weight_ref, position_ref, coarse_ref, fine_ref,
-    dx_ref, own_ref, dw_ref, sum_ref,
-):
-    block = pl.program_id(0)
-    row_count, width = dq_ref.shape
-
-    @pl.when(block == 0)
-    def _():
-        sum_ref[...] = jnp.zeros_like(sum_ref)
-
-    @pl.when(jnp.logical_not(block_active(block, info, row_count)))
-    def _():
-        dx_ref[...] = jnp.zeros_like(dx_ref)
-
-    @pl.when(block_active(block, info, row_count))
-    def _():
-        cosine, sine = rotary(position_ref[pl.ds(block, 1), :], coarse_ref, fine_ref)
-
-        def back(ref):
-            tiles = []
-            for tile in range(width // TILE):
-                cut = slice(tile * TILE, (tile + 1) * TILE)
-                tiles.append(turn_back(ref[:, cut].astype(F32), cosine, sine).astype(BF16))
-            return jnp.concatenate(tiles, axis=1)
-
-        dk = back(dk_ref)
-        dv = dv_ref[...]
-        first = first_ref[...]
-        total = dot(dk, weight_ref[:, width : 2 * width], ((1,), (1,))) + dot(
-            dv, weight_ref[:, 2 * width :], ((1,), (1,))
-        )
-        sum_ref[:, width : 2 * width] += dot(first, dk, ((0,), (0,)))
-        sum_ref[:, 2 * width :] += dot(first, dv, ((0,), (0,)))
-        dx_ref[...] = total.astype(BF16)
-
-        @pl.when(block * BLOCK == info[4])
-        def _():
-            dq = back(dq_ref)
-            sum_ref[:, :width] += dot(first, dq, ((0,), (0,)))
-            own = dot(dq, weight_ref[:, :width], ((1,), (1,)))
-            dx_ref[...] = (total + own).astype(BF16)
-            own_ref[...] = total + own
-
-    @pl.when(block == pl.num_programs(0) - 1)
-    def _():
-        dw_ref[...] = sum_ref[...].astype(BF16)
-
-
-def spread(info, first, dk, dv, dq, weight, positions, tables):
-    row_count, width = dq.shape
-    total = first.shape[0]
-    rows = pl.BlockSpec((BLOCK, width), lambda i, *_: (i, 0))
-
-    def whole(shape):
-        return pl.BlockSpec(shape, lambda i, *_: (0,) * len(shape))
-
-    return pl.pallas_call(
-        spread_kernel,
-        grid_spec=pltpu.PrefetchScalarGridSpec(
-            num_scalar_prefetch=1,
-            grid=(total // BLOCK,),
-            in_specs=[
-                rows, rows, rows, whole(dq.shape), whole(weight.shape), whole(positions.shape),
-                whole(tables[0].shape), whole(tables[1].shape),
-            ],
-            out_specs=[rows, whole(dq.shape), whole(weight.shape)],
-            scratch_shapes=[pltpu.VMEM(weight.shape, F32)],
-        ),
-        out_shape=[
-            jax.ShapeDtypeStruct((total, width), BF16),
-            jax.ShapeDtypeStruct(dq.shape, F32),
-            jax.ShapeDtypeStruct(weight.shape, BF16),
-        ],
-        compiler_params=params(),
-        name="spread",
-    )(info, first, dk, dv, dq, weight, positions, *tables)
-
-
-def finish_kernel(
-    info, grad_ref, x_ref, g_mid_ref, cond_ref, ada_ref, bias_ref, gain_ref,
-    tokens_ref, small_ref, slots_ref,
-):
-    width = x_ref.shape[1]
-    first_row = info[4]
-    mods = dot(cond_ref[...], ada_ref[...]) + bias_ref[...]
-    scale = 1.0 + mods[:, width:]
-    picks = slot_picks(x_ref.shape[0], first_row, info)
-    grad = grad_ref[...].astype(F32)
-    xh, inverse = normed(x_ref[...].astype(F32))
-    slots_ref[:, :width] = slot_sums(first_row, info, grad)
-    moved = grad * xh
-    slots_ref[:, width:] = slot_sums(first_row, info, moved * gain_ref[...])
-    small_ref[0:1, :] = jnp.sum(moved * dot(picks, pick_table(scale)), axis=0, keepdims=True)
-    h = grad * dot(picks, pick_table(scale * gain_ref[...]))
-    tokens_ref[...] = g_mid_ref[...] + inverse * (
-        h - jnp.mean(h, axis=1, keepdims=True) - xh * jnp.mean(h * xh, axis=1, keepdims=True)
-    )
-
-
-def finish(info, grad, x, g_mid, cond, ada, bias, gain):
-    row_count, width = x.shape
-
-    def whole(shape):
-        return pl.BlockSpec(shape, lambda i, *_: (0,) * len(shape))
-
-    return pl.pallas_call(
-        finish_kernel,
-        grid_spec=pltpu.PrefetchScalarGridSpec(
-            num_scalar_prefetch=1,
-            grid=(1,),
-            in_specs=[
-                whole(grad.shape), whole(x.shape), whole(x.shape), whole(cond.shape),
-                whole((ada.shape[0], 2 * width)), whole((1, 2 * width)), whole(gain.shape),
-            ],
-            out_specs=[whole(x.shape), whole((8, width)), whole((8, 2 * width))],
-        ),
-        out_shape=[
-            jax.ShapeDtypeStruct(x.shape, F32),
-            jax.ShapeDtypeStruct((8, width), F32),
-            jax.ShapeDtypeStruct((8, 2 * width), F32),
-        ],
-        compiler_params=params(),
-        name="finish",
-    )(info, grad, x, g_mid, cond, ada, bias, gain)
-
-
 MESH = pl.DeviceIdType.MESH
 
 
 def piece_of(array, which):
     rows, columns = array
-    if rows >= 192:
-        quarter = rows // 4
-        return which * quarter, quarter, 0, columns
     if rows % 32 == 0 and (columns // 2) % TILE == 0:
         return (which % 2) * (rows // 2), rows // 2, (which // 2) * (columns // 2), columns // 2
     return 0, rows, which * (columns // 4), columns // 4
+
+
+def cut_of(start, size, whole, unit):
+    if size == whole:
+        return slice(None)
+    return pl.ds(pl.multiple_of(start, unit), size)
 
 
 class Place:
@@ -941,18 +979,35 @@
         else:
             work()
 
-    sequence = [0, 1, count] + list(range(2, count))
-    for a in sequence:
+    def turned(index):
+        for a in range(count):
+            turn_copy(a, index).wait_recv()
+            next_copy(a, index, 1).start()
+
+    def on_lines(index):
+        for a in range(count):
+            on_line(a, index)
+
+    token_up, token_down = own_pair(count)
+    for a in range(count):
         start_own(a)
-    for a in sequence:
-        for index in range(3):
-            on_line(a, index)
-        if a != count:
-            for index in range(3):
-                turn_copy(a, index).wait_recv()
-                next_copy(a, index, 1).start()
-    for a in range(count):
-        for index in range(3):
+    own_to_sibling(count).start()
+    pl.when(z == 0)(token_up.start)
+    pl.when(z == 3)(token_down.start)
+    on_lines(0)
+    pl.when(z == 1)(token_up.start)
+    pl.when(z == 2)(token_down.start)
+    on_lines(1)
+    turned(0)
+    on_lines(2)
+    pl.when(z == 2)(token_up.start)
+    pl.when(z == 1)(token_down.start)
+    turned(1)
+    turned(2)
+    for index in range(3):
+        on_line(count, index)
+    for index in range(3):
+        for a in range(count):
             next_copy(a, index, 0).wait_recv()
             next_copy(a, index, 1).wait_recv()
             back_copy(a, index).start()
@@ -1026,68 +1081,742 @@
     )(*shards, x, positions, vector)
 
 
+def add_into(target, source):
+    rows = target.shape[-2]
+    step = 32 if rows % 32 == 0 else 16
+    lead = target.shape[:-2]
+
+    @pl.loop(0, rows // step)
+    def _(turn_index):
+        cut = pl.ds(pl.multiple_of(turn_index * step, 16), step)
+        for index in np.ndindex(*lead):
+            at = (*index, cut, slice(None))
+            target[at] = target[at] + source[at]
+
+
+def finish_rows(info, grad, x, g_mid, mods, gain):
+    width = x.shape[1]
+    first_row = info[4]
+    scale = 1.0 + mods[:, width:]
+    picks = slot_picks(x.shape[0], first_row, info)
+    xh, inverse = normed(x.astype(F32))
+    moved = grad * xh
+    sums = jnp.concatenate(
+        [slot_sums(first_row, info, grad), slot_sums(first_row, info, moved * gain)], axis=1
+    )
+    g_gain = jnp.sum(moved * dot(picks, pick_table(scale)), axis=0, keepdims=True)
+    h = grad * dot(picks, pick_table(scale * gain))
+    tokens = g_mid + inverse * (
+        h - jnp.mean(h, axis=1, keepdims=True) - xh * jnp.mean(h * xh, axis=1, keepdims=True)
+    )
+    return tokens, sums, g_gain
+
+
+def folded(values, columns):
+    return jnp.concatenate(
+        [values[:, at : at + columns] for at in range(0, values.shape[1], columns)], axis=0
+    )
+
+
+def reduce_kernel(shapes, summed, size, groups, info, *refs):
+    count, made = len(shapes), summed - 1
+    refs = list(refs)
+    grad_refs = [refs.pop(0) for _ in range(count - 1)]
+    grad_refs.insert(made, None)
+    (
+        first_ref, dk_ref, dv_ref, early_ref, dq_ref, weight_ref, position_ref, coarse_ref, fine_ref,
+        x_ref, g_mid_ref, mods_ref, gain_ref,
+    ) = (refs.pop(0) for _ in range(13))
+    out_refs = [refs.pop(0) for _ in range(count)]
+    tokens_ref, early_all, late_all = (refs.pop(0) for _ in range(3))
+    rest = refs
+    own, turned, nexted, far = ([rest.pop(0) for _ in range(count)] for _ in range(4))
+    side, upward, downward = ([rest.pop(0) for _ in range(summed)] for _ in range(3))
+    (
+        first_in, dk_in, dv_in, dw_sum, made_out, dx_out,
+        dx_own, dx_side, dx_up, dx_down, late_ref, early_in, late_in, early_sum, late_sum,
+        own_sem, side_send, side_recv, turn_send, turn_recv, next_send, next_recv, line_send,
+        line_recv, far_send, far_recv, share_send, share_recv, final_sem,
+        block_sem, dx_side_send, dx_side_recv, dx_send, dx_recv,
+        pack_send, pack_recv, wide_send, wide_recv, pack_own,
+    ) = rest
+    place = Place()
+    z, core, narrow = place.z, place.core, place.narrow
+    barrier = pltpu.get_barrier_semaphore()
+    for step in range(1, size):
+        pl.semaphore_signal(
+            barrier, inc=1, device_id=place.column((narrow + step) % size), device_id_type=MESH
+        )
+    for step in range(1, groups):
+        pl.semaphore_signal(
+            barrier, inc=1, device_id=((place.wide + step) % groups, narrow), device_id_type=MESH
+        )
+    pl.semaphore_wait(barrier, size + groups - 2)
+
+    def remote(source, target, send, recv, device):
+        return pltpu.make_async_remote_copy(
+            src_ref=source, dst_ref=target, send_sem=send, recv_sem=recv, device_id=device,
+            device_id_type=MESH,
+        )
+
+    def piece(ref, a, which, lead):
+        rows, columns = shapes[a]
+        first_row, row_count, first_column, column_count = piece_of(shapes[a], which)
+        return ref.at[
+            (*lead, cut_of(first_row, row_count, rows, 16), cut_of(first_column, column_count, columns, TILE))
+        ]
+
+    quarter = place.quarter
+    other1 = place.flip(quarter, place.bit1)
+    other2 = place.flip(quarter, place.bit2)
+    every = (slice(None),)
+
+    def pack_copies(which, source, target):
+        return [
+            remote(
+                source, target.at[narrow], pack_send.at[which, step], pack_recv.at[which, step],
+                place.column((narrow + step) % size),
+            )
+            for step in range(1, size)
+        ]
+
+    def wide_copies(which, source, target):
+        return [
+            remote(
+                source, target.at[place.wide], wide_send.at[which, step], wide_recv.at[which, step],
+                ((place.wide + step) % groups, narrow),
+            )
+            for step in range(1, groups)
+        ]
+
+    early_copies = pack_copies(0, early_ref, early_in)
+    early_own = pltpu.make_async_copy(early_ref, early_in.at[narrow], pack_own.at[0])
+    early_own.start()
+
+    side_copy, own_copy = [], []
+    for a in range(count):
+        if a == made:
+            side_copy.append(
+                remote(made_out, side[a], side_send.at[a], side_recv.at[a], place.sibling())
+            )
+            own_copy.append(None)
+            continue
+        if a < summed:
+            side_copy.append(
+                remote(grad_refs[a].at[:, 1 - core], side[a], side_send.at[a], side_recv.at[a], place.sibling())
+            )
+            own_copy.append(pltpu.make_async_copy(grad_refs[a].at[:, core], own[a], own_sem.at[a]))
+            side_copy[a].start()
+        else:
+            own_copy.append(pltpu.make_async_copy(grad_refs[a], own[a].at[0], own_sem.at[a]))
+        own_copy[a].start()
+
+    def dx_copy(upwards, slot):
+        zp = jnp.clip(z + 1 + slot if upwards else z - 1 - slot, 0, 3)
+        way = 0 if upwards else 1
+        landing = dx_up if upwards else dx_down
+        return remote(
+            dx_own.at[zp], landing.at[slot], dx_send.at[way, slot], dx_recv.at[way, slot],
+            place.up() if upwards else place.down(),
+        )
+
+    def dx_middle():
+        @pl.when(z < 3)
+        def _():
+            @pl.when(z > 0)
+            def _():
+                dx_copy(True, 1).wait_recv()
+                add_into(dx_own.at[jnp.minimum(z + 1, 3)], dx_up.at[1])
+
+            dx_copy(True, 0).start()
+
+        @pl.when(z > 0)
+        def _():
+            @pl.when(z < 3)
+            def _():
+                dx_copy(False, 1).wait_recv()
+                add_into(dx_own.at[jnp.maximum(z - 1, 0)], dx_down.at[1])
+
+            dx_copy(False, 0).start()
+
+    def dx_end():
+        @pl.when(z > 0)
+        def _():
+            dx_copy(True, 0).wait_recv()
+            add_into(dx_own.at[z], dx_up.at[0])
+
+        @pl.when(z < 3)
+        def _():
+            dx_copy(False, 0).wait_recv()
+            add_into(dx_own.at[z], dx_down.at[0])
+
+        pl.when(z < 3)(dx_copy(True, 0).wait_send)
+        pl.when(z < 2)(dx_copy(True, 1).wait_send)
+        pl.when(z > 0)(dx_copy(False, 0).wait_send)
+        pl.when(z > 1)(dx_copy(False, 1).wait_send)
+
+    def turn_copy(a):
+        rows, columns = shapes[a]
+        out = []
+        for bit in (1, 2):
+            if bit == 1:
+                there = (slice(None), pl.ds(pl.multiple_of((1 - quarter % 2) * (rows // 2), 16), rows // 2), slice(None))
+                landing = turned[a].at[:, pl.ds(0, rows // 2), :]
+            else:
+                there = (slice(None), slice(None), pl.ds(pl.multiple_of((1 - quarter // 2) * (columns // 2), TILE), columns // 2))
+                landing = turned[a].at[:, :, pl.ds(0, columns // 2)]
+            out.append(
+                remote(own[a].at[there], landing, turn_send.at[a], turn_recv.at[a], place.partner(bit))
+            )
+        return out
+
+    def by_core(copies, what):
+        pl.when(core == 0)(getattr(copies[0], what))
+        pl.when(core == 1)(getattr(copies[1], what))
+
+    def join(a):
+        if a != made:
+            own_copy[a].wait()
+        if a < summed:
+            side_copy[a].wait_recv()
+            add_into(own[a], side[a])
+
+    def start_turn(a):
+        by_core(turn_copy(a), "start")
+
+    def next_copy(a):
+        return remote(
+            piece(own[a], a, other2, every), nexted[a], next_send.at[a], next_recv.at[a],
+            place.partner(place.bit2),
+        )
+
+    def start_next(a):
+        rows, columns = shapes[a]
+        by_core(turn_copy(a), "wait_recv")
+
+        @pl.when(core == 0)
+        def _():
+            add_into(
+                own[a].at[:, pl.ds(pl.multiple_of((quarter % 2) * (rows // 2), 16), rows // 2), :],
+                turned[a].at[:, pl.ds(0, rows // 2), :],
+            )
+
+        @pl.when(core == 1)
+        def _():
+            add_into(
+                own[a].at[:, :, pl.ds(pl.multiple_of((quarter // 2) * (columns // 2), TILE), columns // 2)],
+                turned[a].at[:, :, pl.ds(0, columns // 2)],
+            )
+
+        next_copy(a).start()
+
+    def line_copy(a, zp, upwards, source):
+        if upwards:
+            return remote(source, upward[a].at[zp], line_send.at[a, zp, 0], line_recv.at[a, zp, 0], place.up())
+        return remote(source, downward[a].at[zp], line_send.at[a, zp, 1], line_recv.at[a, zp, 1], place.down())
+
+    def start_line(a):
+        next_copy(a).wait_recv()
+        add_into(piece(own[a], a, quarter, every), nexted[a])
+        if a >= summed:
+            return
+        for zp in (3, 2, 1):
+            pl.when(z == 0)(line_copy(a, zp, True, piece(own[a], a, quarter, (zp,))).start)
+            low = 3 - zp
+            pl.when(z == 3)(line_copy(a, low, False, piece(own[a], a, quarter, (low,))).start)
+
+    def middle_line(a):
+        if a >= summed:
+            return
+        for zp in (3, 2, 1):
+
+            @pl.when(jnp.logical_and(z > 0, z < zp))
+            def _():
+                copy = line_copy(a, zp, True, upward[a].at[zp])
+                copy.wait_recv()
+                add_into(upward[a].at[zp], piece(own[a], a, quarter, (zp,)))
+                copy.start()
+
+            low = 3 - zp
+
+            @pl.when(jnp.logical_and(z < 3, z > low))
+            def _():
+                copy = line_copy(a, low, False, downward[a].at[low])
+                copy.wait_recv()
+                add_into(downward[a].at[low], piece(own[a], a, quarter, (low,)))
+                copy.start()
+
+    def share_copy(a, which, bit_place, slot):
+        source = piece(out_refs[a], a, which, ())
+        return remote(source, source, share_send.at[a, slot], share_recv.at[a, slot], place.partner(bit_place))
+
+    def kept(a):
+        return piece(own[a], a, quarter, (z,) if a < summed else (0,))
+
+    def final_copy(a):
+        return pltpu.make_async_copy(
+            kept(a), piece(out_refs[a], a, quarter, ()), final_sem.at[a]
+        )
+
+    def far_copy(a, which, bit):
+        return remote(
+            kept(a), far[a].at[which], far_send.at[a, which],
+            far_recv.at[a, which], (place.flip(place.wide, bit), narrow),
+        )
+
+    def end_line(a):
+        mine = kept(a)
+        if a < summed:
+
+            @pl.when(z > 0)
+            def _():
+                line_copy(a, z, True, mine).wait_recv()
+                add_into(mine, upward[a].at[z])
+
+            @pl.when(z < 3)
+            def _():
+                line_copy(a, z, False, mine).wait_recv()
+                add_into(mine, downward[a].at[z])
+
+        bit, which = 4, 0
+        while bit < groups:
+            copy = far_copy(a, which, bit)
+            copy.start()
+            copy.wait()
+            add_into(mine, far[a].at[which])
+            bit, which = bit * 2, which + 1
+        final_copy(a).start()
+
+    def start_share(a):
+        final_copy(a).wait()
+        share_copy(a, quarter, place.bit1, 0).start()
+        share_copy(a, quarter, place.bit2, 1).start()
+
+    def pass_share(a):
+        share_copy(a, quarter, place.bit1, 0).wait_recv()
+        share_copy(a, other1, place.bit2, 2).start()
+
+    def close(a):
+        share_copy(a, quarter, place.bit2, 1).wait_recv()
+        share_copy(a, other1, place.bit2, 2).wait_recv()
+        share_copy(a, quarter, place.bit1, 0).wait_send()
+        share_copy(a, quarter, place.bit2, 1).wait_send()
+        share_copy(a, other1, place.bit2, 2).wait_send()
+        by_core(turn_copy(a), "wait_send")
+        next_copy(a).wait_send()
+        if a >= summed:
+            return
+        side_copy[a].wait_send()
+        for zp in range(4):
+            mine = piece(own[a], a, quarter, (zp,))
+            pl.when(z < zp)(line_copy(a, zp, True, mine).wait_send)
+            pl.when(z > zp)(line_copy(a, zp, False, mine).wait_send)
+
+    def column_total(landed):
+        total = landed[0].astype(F32)
+        for step in range(1, size):
+            total = total + landed[step].astype(F32)
+        return total.astype(BF16)
+
+    width = x_ref.shape[1]
+    block_rows = x_ref.shape[0]
+
+    def zp_of(step):
+        near = place.near
+        return jnp.where(
+            step == 0, (z + 2) % 4, jnp.where(step == 1, near, jnp.where(step == 2, (near + 2) % 4, z))
+        )
+
+    def needed(step):
+        zp = zp_of(step)
+        return jnp.logical_and(zp - z < 3, z - zp < 3)
+
+    def fetch(turn_index):
+        parity = turn_index % 2
+        owner = zp_of(turn_index // 2) * 2 + jnp.where(parity == 0, 1 - core, core)
+        rows = pl.ds(pl.multiple_of(owner * block_rows, block_rows), block_rows)
+        return [
+            pltpu.make_async_copy(ref.at[rows, :], landing.at[parity], block_sem.at[which, parity])
+            for which, (ref, landing) in enumerate(((first_ref, first_in), (dk_ref, dk_in), (dv_ref, dv_in)))
+        ]
+
+    def dx_side_copy(step):
+        return remote(
+            dx_out.at[step % 2], dx_side.at[zp_of(step)], dx_side_send.at[step], dx_side_recv.at[step],
+            place.sibling(),
+        )
+
+    def turned_back(values, cosine, sine):
+        tiles = []
+        for tile in range(width // TILE):
+            cut = slice(tile * TILE, (tile + 1) * TILE)
+            tiles.append(turn_back(values[:, cut].astype(F32), cosine, sine).astype(BF16))
+        return jnp.concatenate(tiles, axis=1)
+
+    dw_sum[...] = jnp.zeros_like(dw_sum)
+    for copy in fetch(0):
+        copy.start()
+
+    @pl.loop(0, 8)
+    def _(turn_index):
+        step = turn_index // 2
+        parity = turn_index % 2
+        zp = zp_of(step)
+        owner = zp * 2 + jnp.where(parity == 0, 1 - core, core)
+
+        @pl.when(turn_index < 7)
+        def _():
+            for copy in fetch(turn_index + 1):
+                copy.start()
+
+        for copy in fetch(turn_index):
+            copy.wait()
+
+        @pl.when(needed(step))
+        def _():
+            cosine, sine = rotary(position_ref[owner], coarse_ref, fine_ref)
+            dk = turned_back(dk_in[parity], cosine, sine)
+            dv = dv_in[parity]
+            first = first_in[parity]
+            dw_sum[:, width : 2 * width] += dot(first, dk, ((0,), (0,)))
+            dw_sum[:, 2 * width :] += dot(first, dv, ((0,), (0,)))
+            total = (
+                dot(dk, weight_ref[:, width : 2 * width], ((1,), (1,)))
+                + dot(dv, weight_ref[:, 2 * width :], ((1,), (1,)))
+            ).astype(BF16)
+
+            @pl.when(parity == 0)
+            def _():
+                @pl.when(jnp.logical_and(step > 1, needed(step - 2)))
+                def _():
+                    dx_side_copy(step - 2).wait_send()
+
+                dx_out[step % 2] = total
+                dx_side_copy(step).start()
+
+            @pl.when(parity == 1)
+            def _():
+                dx_own[zp] = total
+                dx_side_copy(step).wait_recv()
+                add_into(dx_own.at[zp], dx_side.at[zp])
+
+        @pl.when(turn_index == 1)
+        def _():
+            pl.when(z < 2)(dx_copy(True, 1).start)
+            pl.when(z > 1)(dx_copy(False, 1).start)
+            join(0)
+            start_turn(0)
+
+        @pl.when(turn_index == 3)
+        def _():
+            for a in range(1, count):
+                if a != made:
+                    join(a)
+                    start_turn(a)
+
+    cosine, sine = rotary(position_ref[narrow], coarse_ref, fine_ref)
+    dq = turned_back(dq_ref[...], cosine, sine)
+    dw_sum[:, :width] = dot(first_in[1], dq, ((0,), (0,)))
+    dx_own[z] = (
+        dx_own[z].astype(F32) + dot(dq, weight_ref[:, :width], ((1,), (1,)))
+    ).astype(BF16)
+    shard_rows = shapes[made][0]
+
+    @pl.loop(0, 4)
+    def _(zp):
+        mine = pl.ds(pl.multiple_of((2 * zp + core) * shard_rows, 16), shard_rows)
+        other = pl.ds(pl.multiple_of((2 * zp + 1 - core) * shard_rows, 16), shard_rows)
+        own[made][zp] = dw_sum[mine, :].astype(BF16)
+        made_out[zp] = dw_sum[other, :].astype(BF16)
+
+    side_copy[made].start()
+    dx_middle()
+    for a in range(count):
+        if a != made:
+            start_next(a)
+    join(made)
+    start_turn(made)
+    for copy in early_copies:
+        copy.start()
+    for a in range(made):
+        start_line(a)
+    for a in range(summed, count):
+        start_line(a)
+        end_line(a)
+        start_share(a)
+    for a in range(made):
+        middle_line(a)
+    start_next(made)
+    dx_end()
+    for a in range(made):
+        end_line(a)
+        start_share(a)
+    start_line(made)
+    tokens, sums, g_gain = finish_rows(
+        info, dx_own[z].astype(F32), x_ref[...], g_mid_ref[...], mods_ref[...], gain_ref[...]
+    )
+    tokens_ref[...] = tokens
+    quarter_width = sums.shape[1] // 4
+    late_ref[...] = jnp.concatenate(
+        [
+            folded(sums[:4], quarter_width),
+            folded(g_gain, quarter_width),
+            jnp.zeros((14, quarter_width), F32),
+        ],
+        axis=0,
+    ).astype(BF16)
+    late_copies = pack_copies(1, late_ref, late_in)
+    for copy in late_copies:
+        copy.start()
+    late_own = pltpu.make_async_copy(late_ref, late_in.at[narrow], pack_own.at[1])
+    late_own.start()
+    middle_line(made)
+    for a in range(count):
+        if a != made:
+            pass_share(a)
+    end_line(made)
+    start_share(made)
+    for copy in early_copies:
+        copy.wait_recv()
+    early_own.wait()
+    early_sum[...] = column_total(early_in)
+    early_wide = wide_copies(0, early_sum, early_all)
+    for copy in early_wide:
+        copy.start()
+    early_final = pltpu.make_async_copy(early_sum, early_all.at[place.wide], pack_own.at[2])
+    early_final.start()
+    for copy in late_copies:
+        copy.wait_recv()
+    late_own.wait()
+    late_sum[...] = column_total(late_in)
+    late_wide = wide_copies(1, late_sum, late_all)
+    for copy in late_wide:
+        copy.start()
+    late_final = pltpu.make_async_copy(late_sum, late_all.at[place.wide], pack_own.at[3])
+    late_final.start()
+    pass_share(made)
+    for a in range(count):
+        close(a)
+    for step in (2, 3):
+        pl.when(needed(step))(dx_side_copy(step).wait_send)
+    pl.when(jnp.logical_and(needed(0), jnp.logical_not(needed(2))))(dx_side_copy(0).wait_send)
+    pl.when(jnp.logical_and(needed(1), jnp.logical_not(needed(3))))(dx_side_copy(1).wait_send)
+    early_final.wait()
+    late_final.wait()
+    for copy in early_copies + late_copies:
+        copy.wait_send()
+    for copy in early_wide + late_wide:
+        copy.wait()
+
+
+def reduce_all(
+    info, grads, summed, first, dk, dv, early, dq, weight, positions, tables, x, g_mid, mods, gain,
+    size, groups,
+):
+    shapes = tuple((grad.shape[0] // size, grad.shape[1]) for grad in (*grads, weight)) + tuple(
+        shard.shape for shard in summed
+    )
+    count, full = len(shapes), len(grads) + 1
+    row_count, width = x.shape
+    anywhere = pl.BlockSpec(memory_space=pl.ANY)
+    vmem = pl.BlockSpec(memory_space=pltpu.VMEM)
+    dma = pltpu.SemaphoreType.DMA
+
+    def scratch(*shape):
+        return pltpu.VMEM(shape, BF16)
+
+    pieces = [(piece_of(shape, 0)[1], piece_of(shape, 0)[3]) for shape in shapes]
+    leads = [4] * full + [1] * len(summed)
+    late = (32, 2 * width // 4)
+    turns = max(1, int(math.log2(groups)) - 2)
+    scratch_shapes = (
+        [scratch(lead, *shape) for lead, shape in zip(leads, shapes)]
+        + [scratch(lead, *shape) for lead, shape in zip(leads, shapes)]
+        + [scratch(lead, *piece) for lead, piece in zip(leads, pieces)]
+        + [scratch(turns, *piece) for piece in pieces]
+        + [scratch(4, *shape) for shape in shapes[:full]]
+        + [scratch(4, *piece) for piece in pieces[:full]] * 2
+        + [
+            scratch(2, row_count, width), scratch(2, row_count, width),
+            scratch(2, row_count, width), pltpu.VMEM(weight.shape, F32),
+            scratch(4, *shapes[full - 1]), scratch(2, row_count, width),
+            scratch(4, row_count, width), scratch(4, row_count, width),
+            scratch(2, row_count, width), scratch(2, row_count, width),
+            scratch(*late), scratch(size, *early.shape), scratch(size, *late),
+            scratch(*early.shape), scratch(*late),
+            dma((count,)), dma((count,)), dma((count,)), dma((count,)), dma((count,)),
+            dma((count,)), dma((count,)), dma((count, 4, 2)), dma((count, 4, 2)),
+            dma((count, turns)), dma((count, turns)), dma((count, 3)), dma((count, 3)),
+            dma((count,)), dma((3, 2)), dma((4,)), dma((4,)), dma((2, 2)), dma((2, 2)),
+            dma((2, size)), dma((2, size)), dma((2, groups)), dma((2, groups)), dma((4,)),
+        ]
+    )
+    views = [grad.reshape(4, 2, *shape) for grad, shape in zip(grads, shapes)]
+    return pl.pallas_call(
+        functools.partial(reduce_kernel, shapes, full, size, groups),
+        out_shape=[jax.ShapeDtypeStruct(shape, BF16) for shape in shapes]
+        + [
+            jax.ShapeDtypeStruct(x.shape, F32),
+            jax.ShapeDtypeStruct((groups, *early.shape), BF16),
+            jax.ShapeDtypeStruct((groups, *late), BF16),
+        ],
+        in_specs=[pl.BlockSpec(memory_space=pltpu.SMEM)]
+        + [anywhere] * (count + 3)
+        + [vmem] * 9,
+        out_specs=[anywhere] * count + [vmem, anywhere, anywhere],
+        scratch_shapes=scratch_shapes,
+        compiler_params=pltpu.CompilerParams(
+            collective_id=2, has_side_effects=True, vmem_limit_bytes=REDUCE_VMEM
+        ),
+        name="reduce_all",
+        )(
+        info, *views, *summed, first, dk, dv, early, dq, weight, positions, *tables, x, g_mid, mods, gain,
+    )
+
+
+def tail_kernel(
+    g0_ref, g1_ref, g2_ref, g3_ref, early_ref, late_ref, time_ref, ada_ref,
+    o0_ref, o1_ref, o2_ref, o3_ref, g_ada_ref, g_bias_ref, g_time_ref, norm1_ref, norm2_ref, fc1_b_ref,
+    fc2_b_ref, mod_ref, cond_ref, turned_ref, full_ref,
+):
+    for source, target in ((g0_ref, o0_ref), (g1_ref, o1_ref), (g2_ref, o2_ref), (g3_ref, o3_ref)):
+        target[...] = source[...].astype(F32)
+    me = lax.axis_index("narrow")
+    groups, _, width = early_ref.shape
+    seqs = time_ref.shape[0]
+    vectors = jnp.zeros((16, width), F32)
+    norm1 = jnp.zeros((2, width // 2), F32)
+    picks = []
+    for group in range(groups):
+        early = early_ref[group].astype(F32)
+        late = late_ref[group].astype(F32)
+        vectors = vectors + early[16:32]
+        norm1 = norm1 + late[16:18]
+        rows = jnp.concatenate(
+            [late[4 * at : 4 * at + 4] for at in range(4)] + [early[4 * at : 4 * at + 4] for at in range(4)],
+            axis=1,
+        )
+        mod_ref[4 * group : 4 * group + 4, :] = rows
+        sub = lax.broadcasted_iota(jnp.int32, (seqs, TILE), 0).astype(F32)
+        lane = lax.broadcasted_iota(jnp.int32, (seqs, TILE), 1)
+        pick = jnp.where(jnp.logical_and(sub == early[22:23, :TILE], lane < 4), 1.0, 0.0)
+        picks.append(pick)
+        cond_ref[4 * group : 4 * group + 4, :] = dot(
+            pick.astype(BF16), time_ref[...], ((0,), (0,))
+        )[:4]
+    g_mod = mod_ref[...]
+
+    def mine(row, size):
+        lanes = row.shape[1]
+        block = jnp.broadcast_to(row, (8, lanes))
+        return pltpu.roll(block, lax.rem(lanes - me * size, lanes), 1)[:1, :size]
+
+    g_bias_ref[...] = mine(jnp.sum(g_mod, axis=0, keepdims=True), g_bias_ref.shape[1])
+    norm1_ref[...] = mine(jnp.concatenate([norm1[0:1], norm1[1:2]], axis=1), norm1_ref.shape[1])
+    norm2_ref[...] = mine(vectors[0:1], norm2_ref.shape[1])
+    fc2_b_ref[...] = mine(vectors[1:2], fc2_b_ref.shape[1])
+    fc1_b_ref[...] = mine(
+        jnp.concatenate([vectors[2 + at : 3 + at] for at in range(4)], axis=1), fc1_b_ref.shape[1]
+    )
+    turned_ref[...] = cond_ref[...].T
+    own_rows = g_ada_ref.shape[0]
+    g_ada_ref[...] = dot(
+        turned_ref[pl.ds(pl.multiple_of(me * own_rows, 8), own_rows), :], g_mod, precision=HIGH
+    )
+    g_cond = dot(g_mod, ada_ref[...].astype(F32), ((1,), (1,)), precision=HIGH)
+    total = jnp.zeros((seqs, TILE), F32)
+    for group in range(groups):
+        part = jnp.concatenate([g_cond[4 * group : 4 * group + 4], jnp.zeros((TILE - 4, TILE), F32)], axis=0)
+        total = total + dot(picks[group], part, precision=HIGH)
+    full_ref[...] = total
+    own_seqs = g_time_ref.shape[0]
+    g_time_ref[...] = full_ref[pl.ds(me * own_seqs, own_seqs), :]
+
+
+def tail(grads, early, late, time_emb, ada, sizes):
+    vmem = pl.BlockSpec(memory_space=pltpu.VMEM)
+    groups = early.shape[0]
+    devices = ada.shape[1] // sizes[2]
+    return pl.pallas_call(
+        tail_kernel,
+        out_shape=[jax.ShapeDtypeStruct(grad.shape, F32) for grad in grads]
+        + [
+            jax.ShapeDtypeStruct((ada.shape[0] // devices, ada.shape[1]), F32),
+            jax.ShapeDtypeStruct((1, sizes[2]), F32),
+            jax.ShapeDtypeStruct((time_emb.shape[0] // devices, time_emb.shape[1]), F32),
+        ]
+        + [jax.ShapeDtypeStruct((1, sizes[which]), F32) for which in (0, 1, 3, 4)],
+        in_specs=[vmem] * (len(grads) + 4),
+        out_specs=[vmem] * (len(grads) + 7),
+        scratch_shapes=[
+            pltpu.VMEM((4 * groups, ada.shape[1]), F32),
+            pltpu.VMEM((4 * groups, ada.shape[0]), F32),
+            pltpu.VMEM((ada.shape[0], 4 * groups), F32),
+            pltpu.VMEM(time_emb.shape, F32),
+        ],
+        compiler_params=pltpu.CompilerParams(vmem_limit_bytes=VMEM_LIMIT),
+        name="tail",
+    )(*grads, early, late, time_emb, ada)
+
+
 def body(
     tokens, cotangent, time_emb, seq_table, lengths, positions, norm1_gain, norm2_gain,
     ada_weight, ada_bias, qkv_weight, out_weight, fc1_weight, fc1_bias, fc2_weight, fc2_bias,
 ):
     row_count, width = tokens.shape
     me = lax.axis_index("narrow")
-    first_row = me * row_count
+    size, groups = lax.axis_size("narrow"), lax.axis_size("wide")
     slots = lengths.shape[1]
-    below = np.tril(np.ones((slots, slots), np.int32))
-    seq_ends = jnp.sum(jnp.asarray(below) * lengths[0][None, :], axis=1)
-    info = jnp.concatenate(
-        [seq_ends, first_row[None], jnp.zeros((3,), jnp.int32)]
+    below = np.zeros((16, slots), np.int32)
+    below[:slots] = np.tril(np.ones((slots, slots), np.int32))
+    table = np.zeros((16, slots), np.int32)
+    table[8 : 8 + slots] = np.eye(slots, dtype=np.int32)
+    info = (
+        jnp.sum(
+            jnp.asarray(below) * lengths[0][None, :]
+            + jnp.asarray(table) * jnp.where(me == 0, seq_table, 0)[None, :],
+            axis=1,
+        )
+        + (jnp.arange(16) == 4) * (me * row_count)
     ).astype(jnp.int32)
+    seqs = jnp.pad(seq_table, (0, 8 - slots), constant_values=-1)
     onehot_table = (
-        seq_table[:, None] == jnp.arange(time_emb.shape[0], dtype=jnp.int32)[None, :]
+        seqs[:, None] == jnp.arange(time_emb.shape[0], dtype=jnp.int32)[None, :]
     ).astype(BF16)
-    cond = jnp.dot(onehot_table, time_emb, preferred_element_type=F32).astype(BF16)
-    cond8 = jnp.concatenate([cond, jnp.zeros_like(cond)], axis=0)
+    cond8 = jnp.dot(onehot_table, time_emb, preferred_element_type=F32).astype(BF16)
     tables = tuple(jnp.asarray(t) for t in rotary_constants())
-
     pieces = (norm1_gain, norm2_gain, ada_bias, fc1_bias, fc2_bias)
-    cuts = np.cumsum([piece.size for piece in pieces])
-    room = -cuts[-1] % (16 * TILE)
-    vector = jnp.concatenate([*pieces, jnp.zeros((room,), BF16)]).reshape(16, TILE)
-    ada, qkv_w, out_w, fc1, fc2, x_all, position_all, vectors = gather_all(
-        tokens, positions.reshape(-1, TILE), vector,
-        (ada_weight, qkv_weight, out_weight, fc1_weight, fc2_weight), lax.axis_size("narrow"),
-    )
-    vectors = vectors.reshape(vectors.shape[0], -1)
-    position_all = position_all.reshape(position_all.shape[0], -1)
-    gain1, gain2, bias, fc1_b, fc2_b = (
-        piece.reshape(1, -1).astype(F32) for piece in jnp.split(vectors[:, : cuts[-1]], cuts[:-1], axis=1)
-    )
-
-    keys, values, first, queries = project(
-        info, x_all, position_all, cond8, ada, bias, gain1, qkv_w, tables, row_count
-    )
-    attended, mass = attend(info, queries, keys, values)
-    layer_out, g_fc1, g_fc2, g_fc1_b, g_out, g_att, g_mid, small2, slots2 = mlp(
+    sizes = tuple(piece.size for piece in pieces)
+
+    def spread_gather(shard):
+        part = shard.shape[0] // groups
+        mine = lax.dynamic_slice_in_dim(shard, lax.axis_index("wide") * part, part, 0)
+        return lax.all_gather(mine, ("narrow", "wide"), axis=0, tiled=True)
+
+    out_w, fc1 = (spread_gather(shard) for shard in (out_weight, fc1_weight))
+    ada, qkv_w, fc2, x_all, position_all, vectors = gather_all(
+        tokens, positions.reshape(-1, TILE), packed(pieces), (ada_weight, qkv_weight, fc2_weight), size
+    )
+    keys, values, first, queries, norms, mods1, gain1, gain2, bias, fc1_b, fc2_b = project(
+        info, x_all, position_all, cond8, ada, vectors, sizes, qkv_w, tables, row_count
+    )
+    attended, mass = attend(info, queries, keys, values, norms)
+    layer_out, g_fc1, g_fc2, g_out, g_att, g_mid, early = mlp(
         info, tokens, attended, cotangent, cond8, ada, bias, gain2, out_w, fc1, fc1_b, fc2, fc2_b
     )
     dq, dk, dv = attend_back(info, queries, keys, values, g_att, attended, mass)
-    dx, own, g_qkv = spread(info, first, dk, dv, dq, qkv_w, position_all, tables)
-    grad_first = lax.psum_scatter(dx, "narrow", scatter_dimension=0, tiled=True)
-    grad_tokens, small1, slots1 = finish(
-        info, grad_first, tokens, g_mid, cond8, ada, bias, gain1
-    )
-    grad_slot = jnp.concatenate([slots1[:slots], slots2[:slots]], axis=1)
-    grad_ada_bias = jnp.sum(grad_slot, axis=0)
-    grad_ada = jnp.einsum("sc,se->ce", cond.astype(F32), grad_slot, precision=HIGH)
-    grad_cond = jnp.einsum("se,ce->sc", grad_slot, ada.astype(F32), precision=HIGH)
-    grad_time = jnp.einsum("sn,sc->nc", onehot_table.astype(F32), grad_cond, precision=HIGH)
-    partial = (
-        grad_time, small1[0], small2[1], grad_ada, grad_ada_bias, g_qkv, g_out, g_fc1,
-        g_fc1_b[0], g_fc2, small2[0],
-    )
-    shards = tuple(
-        lax.psum_scatter(part.astype(BF16), "narrow", scatter_dimension=0, tiled=True)
-        for part in partial
-    )
-    sums = jax.tree.map(lambda part: part.astype(F32), lax.psum(shards, "wide"))
-    return (layer_out, grad_tokens) + tuple(sums)
+    g_fc1 = lax.psum_scatter(g_fc1, "narrow", scatter_dimension=0, tiled=True)
+    g_fc2, g_out, g_qkv, g_fc1, grad_tokens, early_all, late_all = reduce_all(
+        info, (g_fc2, g_out), (g_fc1,), first, dk, dv, early, dq, qkv_w, position_all, tables, tokens,
+        g_mid, mods1, gain1, size, groups,
+    )
+    g_fc2, g_out, g_qkv, g_fc1, g_ada, g_ada_bias, g_time, g_norm1, g_norm2, g_fc1_b, g_fc2_b = tail(
+        (g_fc2, g_out, g_qkv, g_fc1), early_all, late_all, time_emb, ada, sizes
+    )
+    return (
+        layer_out, grad_tokens, g_time, g_norm1[0], g_norm2[0], g_ada, g_ada_bias[0], g_qkv, g_out,
+        g_fc1, g_fc1_b[0], g_fc2, g_fc2_b[0],
+    )
 
 
 def solution(mesh):

time: 730 us -> 375 us (0.51)
  waiting for transfers between devices: 334 us -> 49 us
  blocking collectives: 36.2 us -> 0 us
  Pallas kernels: 307 us -> 295 us
  local copies, waits for them, and re-layouts: 12.9 us -> 3.95 us
    reduce_scatter x6 -> x1, waiting for transfers between devices: 306 us -> 42.7 us  [body(): g_fc1 = lax.psum_scatter(g_fc1, 'narrow', scatter_dimension=0, tiled=True)]
    pallas_call x3, Pallas kernels: 51.7 us -> 136 us  [the longest x1 115 us: reduce_all(): pl.pallas_call(functools.partial(reduce_kernel, shapes, full, size, group...]
    pallas_call x1, Pallas kernels: 113 us -> 77.1 us  [gather_all(): pl.pallas_call(functools.partial(gather_kernel, shapes, size), out_shape=...]
    pallas_call x1, Pallas kernels: 54.4 us -> 23.3 us  [attend(): pl.pallas_call(attend_kernel, grid_spec=pltpu.PrefetchScalarGridSpec(num_...]
    pallas_call x1, Pallas kernels: 56.5 us -> 27.6 us  [attend_back(): pl.pallas_call(attend_back_kernel, grid_spec=pltpu.PrefetchScalarGridSpec...]
    unnamed x1 -> x0, blocking collectives: 26.1 us -> none
    psum x1 -> x0, waiting for transfers between devices: 25.1 us -> none  [body(): sums = jax.tree.map(lambda part: part.astype(F32), lax.psum(shards, 'wide'))]
    convert_element_type x14 -> x0, other arithmetic: 10.2 us -> none  [the longest x11 9.97 us: body(): sums = jax.tree.map(lambda part: part.astype(F32), lax.psum(shards, 'wide'))]
  transfers between devices with their start and end apart: 7 -> 3, of which waited for: 7 -> 2; matrix products, arithmetic and copies ran while one was open for 1% -> 2% of each run, Pallas kernels for 1% -> 38%
where the time goes in v2:
time: 375 us; the launch traced here: 370 us
  Pallas kernels  295 us (79%)
  waiting for transfers between devices  49 us (13%)
  between operations  14.2 us (4%)
  other arithmetic  5.83 us (2%)
  local copies, waits for them, and re-layouts  3.95 us (1%)
    pallas_call x1, Pallas kernels, reduce_all(): pl.pallas_call(functools.partial(reduce_kernel, shapes, full, size, group...  115 us
    pallas_call x1, Pallas kernels, gather_all(): pl.pallas_call(functools.partial(gather_kernel, shapes, size), out_shape=...  77.1 us
    reduce_scatter x1, waiting for transfers between devices, body(): g_fc1 = lax.psum_scatter(g_fc1, 'narrow', scatter_dimension=0, tiled=True)  42.7 us
    pallas_call x1, Pallas kernels, mlp(): pl.pallas_call(mlp_kernel, grid_spec=pltpu.PrefetchScalarGridSpec(num_sca...  31.3 us
    pallas_call x1, Pallas kernels, attend_back(): pl.pallas_call(attend_back_kernel, grid_spec=pltpu.PrefetchScalarGridSpec...  27.6 us
    pallas_call x1, Pallas kernels, attend(): pl.pallas_call(attend_kernel, grid_spec=pltpu.PrefetchScalarGridSpec(num_...  23.3 us
    pallas_call x1, Pallas kernels, project(): pl.pallas_call(functools.partial(project_kernel, sizes), grid_spec=pltpu....  14.4 us
  transfers between devices with their start and end apart: 3, of which 2 were waited for; matrix products, arithmetic and copies ran while one was open for 2% of the time, Pallas kernels for 38%

profile of v2, /device:TPU:0, one launch (start us, length us, event | category | flops | bytes accessed | tf_op | source)
XLA Modules:
  0.0 369.9 jit_solution(6336613334889850739)
XLA Ops:
  7.2 0.0 all-gather.3.cloned.1.call-start
  7.2 1.4 constant_dynamic-slice_fusion.1
  8.7 0.0 all-gather.5.cloned.1.call-start
  8.8 0.7 constant_dynamic-slice_fusion
  9.5 0.0 reduce-scatter.2.cloned.1.call-start
  9.5 0.7 pad.29
  10.2 1.3 add_bitcast_fusion.refs_5_
  11.5 77.1 %gather_all.1 = (bf16[128,4608]{1,0:T(8,128)(2,1)}, bf16[768,2304]{1,0:T(8,128)(2,1)}, bf16[3072,768]{1,0:T(8,128)(2,1)}, bf16[4096,768]{1,0:T(8,128)(2,1)}, s32...) custom-call(bf16[16,4608]{1,0:T(8,128)(2,1)} %refs_0_.1, bf16[96,2304]{1,0:T(8,128)(2,1)} %refs_1_.1, ...), custom_call_target="tpu_custom_call" | custom-call | tf_op jit(solution)/shard_map/gather_all/pallas_call | solution.py:1059
  88.6 0.7 broadcast_select_fusion
  89.3 0.8 add_reduce_fusion
  90.0 0.5 fusion.1.info
  90.6 1.4 convolution_convert_fusion.cond_ref
  92.0 14.4 %project.1 = (bf16[4096,768]{1,0:T(8,128)(2,1)}, bf16[4096,768]{1,0:T(8,128)(2,1)}, bf16[4096,768]{1,0:T(8,128)(2,1)}, bf16[512,768]{1,0:T(8,128)(2,1)}, f32[8,1...) custom-call(s32[16]{0:T(128)} %fusion.1.info, ...), custom_call_target="tpu_custom_call" | custom-call | tf_op jit(solution)/shard_map/project/pallas_call | solution.py:254
  106.4 23.3 %attend.1 = (f32[512,768]{1,0:T(8,128)}, f32[6,2,512]{2,1,0:T(2,128)}) custom-call(s32[16]{0:T(128)} %fusion.1.info, bf16[512,768]{1,0:T(8,128)(2,1)} %get-tuple-element.65.q_ref, bf16[4096,768]{1,0:T(8,128)(2,1)} %get-tuple-element.66.k_ref, bf16[4096,768]{1,0:T(8,128)(2,1)} %get-tuple-element.67.v_ref, f32[8,128]{1,0:T(8,128)} %get-tuple-element.68.norm_ref), custom_call_target="tpu_custom_call" | custom-call | tf_op jit(solution)/shard_map/attend/pallas_call | solution.py:452
  129.7 6.2 %all-gather.5.cloned.1.call-done.fc1_ref = bf16[768,3072]{1,0:T(8,128)(2,1)} async-done(((bf16[24,3072]{1,0:T(8,128)(2,1)}), bf16[768,3072]{1,0:T(8,128)(2,1)}) %all-gather.5.cloned.1.call-update) | async-done | bytes 4718608 | tf_op jit(solution)/shard_map/all_gather | solution.py:1794
  136.0 31.3 %mlp.1 = (bf16[512,768]{1,0:T(8,128)(2,1)}, bf16[768,3072]{1,0:T(8,128)(2,1)}, bf16[3072,768]{1,0:T(8,128)(2,1)}, bf16[768,768]{1,0:T(8,128)(2,1)}, bf16[512,768...) custom-call(s32[16]{0:T(128)} %fusion.1.info, bf16[512,768]{1,0:T(8,128)(2,1)} %refs_12_.1, ...), custom_call_target="tpu_custom_call" | custom-call | tf_op jit(solution)/shard_map/mlp/pallas_call | solution.py:720
  167.3 0.0 reduce-scatter.2.cloned.1.call-update
  167.3 27.6 %attend_back.1 = (f32[512,768]{1,0:T(8,128)}, bf16[4096,768]{1,0:T(8,128)(2,1)}, bf16[4096,768]{1,0:T(8,128)(2,1)}) custom-call(s32[16]{0:T(128)} %fusion.1.info, bf16[512,768]{1,0:T(8,128)(2,1)} %get-tuple-element.65.q_ref, bf16[4096,768]{1,0:T(8,128)(2,1)} %get-tuple-element.66.k_ref, bf16[4096,768]{1,0:T(8,128)(2,1)} %get-tuple-element.67.v_ref, ...), custom_call_target="tpu_custom_call" | custom-call | tf_op jit(solution)/shard_map/attend_back/pallas_call | solution.py:581
  194.9 42.7 %reduce-scatter.2.cloned.1.call-done.refs_2_ = bf16[96,3072]{1,0:T(8,128)(2,1)} async-done(((bf16[768,3072]{1,0:T(8,128)(2,1)}), bf16[96,3072]{1,0:T(8,128)(2,1)}) %reduce-scatter.2.cloned.1.call-update) | async-done | bytes 589840 | tf_op jit(solution)/shard_map/reduce_scatter | solution.py:1808
  237.6 114.9 %reduce_all.1 = (bf16[384,768]{1,0:T(8,128)(2,1)}, bf16[96,768]{1,0:T(8,128)(2,1)}, bf16[96,2304]{1,0:T(8,128)(2,1)}, bf16[96,3072]{1,0:T(8,128)(2,1)}, f32[512,...) custom-call(s32[16]{0:T(128)} %fusion.1.info, bf16[4,2,384,768]{3,2,1,0:T(8,128)(2,1)} %bitcast.10, ...), custom_call_target="tpu_custom_call" | custom-call | tf_op jit(solution)/shard_map/reduce_all/pallas_call | solution.py:1655
  352.6 6.7 %tail.1 = (f32[384,768]{1,0:T(8,128)}, f32[96,768]{1,0:T(8,128)}, f32[96,2304]{1,0:T(8,128)}, f32[96,3072]{1,0:T(8,128)}, f32[16,4608]{1,0:T(8,128)}, /*index=5*...) custom-call(bf16[384,768]{1,0:T(8,128)(2,1)} %get-tuple-element.90.g, ...), custom_call_target="tpu_custom_call" | custom-call | tf_op jit(solution)/shard_map/tail/pallas_call | solution.py:1740
  359.3 1.3 reduce
  360.6 1.2 reduce.1
  361.8 1.1 copy.34
  (9 shorter events, 0.1 us)
Async XLA Ops:
  7.2 1.6 copy-start
  7.2 122.5 %all-gather.3.cloned.1.call-start = ((), (), s32[]{:S(2)}) async-start(), calls=%async_computation.1 | async-start | bytes 1216512 | tf_op jit(solution)/shard_map/all_gather | solution.py:1794
  8.7 127.2 %all-gather.5.cloned.1.call-start = ((), (), s32[]{:S(2)}) async-start(), calls=%async_computation.2 | async-start | bytes 4866048 | tf_op jit(solution)/shard_map/all_gather | solution.py:1794
  9.5 228.1 %reduce-scatter.2.cloned.1.call-start = ((), (), s32[]{:S(2)}) async-start(), calls=%async_computation.3 | async-start | bytes 5308416 | tf_op jit(solution)/shard_map/reduce_scatter | solution.py:1808
  237.6 125.3 %copy-start.1 = (bf16[96,3072]{1,0:T(8,128)(2,1)S(1)}, bf16[96,3072]{1,0:T(8,128)(2,1)}, u32[]{:S(2)}) copy-start(bf16[96,3072]{1,0:T(8,128)(2,1)} %param.32) | copy-start | bytes 1769476
  352.6 9.2 %copy-start.2 = (f32[512,768]{1,0:T(8,128)S(1)}, f32[512,768]{1,0:T(8,128)}, u32[]{:S(2)}) copy-start(f32[512,768]{1,0:T(8,128)} %get-tuple-element.121) | copy-start | bytes 4718596
Sparse Core Ops, SparseCore 0:
  11.5 58.4 all-gather.2
  73.4 62.5 all-gather.4
  167.4 70.1 reduce-scatter.1
